TPU v7x, 32 devices: a whole 2x2x4 slice. The times are simulated.
32 devices in a mesh: user: 8 (over z, x), item: 4 (over y, core).
Axes of the slice: x: 2, y: 2, z: 4, core: 2. Of those that a mesh axis runs over, the one named last changes fastest.
Arguments:
- xtiles: bfloat16 [8, 96, 256, 256], P('user', 'item'), may hold values from -6 to 6
- row_bits: int32 [8, 96, 8], P('user', 'item'), may hold values from -2147483648 to 2147483646
- col_bits: int32 [8, 96, 8], P('user', 'item'), may hold values from -2147483648 to 2147483646
- tile_row: int32 [8, 96], P('user', 'item'), may hold values from 0 to 1
- tile_col: int32 [8, 96], P('user', 'item'), may hold values from 0 to 3, as said below
- tile_count: int32 [8, 4], P('user', 'item'), may hold values from 1 to 24, as said below
- user_panel: bfloat16 [4096, 256], P('user'), may hold values from -0.375 to 0.375
- item_panel: bfloat16 [1024, 256], P('item'), may hold values from -6 to 6
- test_panel: bfloat16 [1024, 256], P('item'), may hold values from -0.109375 to 0.109375
Outputs:
- sketch: float32 [4096, 256], P('user')
- second_sketch: float32 [4, 256, 256], P('item', 'user')
Inputs may be any that keep to these rules, and one draw needn't show every extreme that they name: `tile_col`: the item block of slot j on user index u is j // 24 - 1, j // 24 or j // 24 + 1, taken modulo 4. `tile_count`: some device has all 24 slots live.
All inputs are finite; a program needn't handle non-finite values.
Results may differ from a plain program's by a relative error of at most 0.0022.
Values may be sent and summed in bfloat16 or wider, within the bound.
A program may use at most 64 MiB of HBM per device.

v0:
```python
import math

import jax
import jax.numpy as jnp
from jax import lax
from jax.sharding import PartitionSpec as P


def padded_2(x, sides, width):
    for axis, dim in sides:
        size, length = (lax.axis_size(axis), x.shape[dim])
        up = [(i, (i + 1) % size) for i in range(size)]
        down = [(j, i) for i, j in up]
        last = lax.slice_in_dim(x, length - width, length, axis=dim)
        first = lax.slice_in_dim(x, 0, width, axis=dim)
        before = lax.ppermute(last, axis, up)
        after = lax.ppermute(first, axis, down)
        x = jnp.concatenate([before, x, after], axis=dim)
    return x


def shifted(block, axis, distance):
    devices = range(lax.axis_size(axis))
    route = [((i - distance) % len(devices), i) for i in devices]
    return lax.ppermute(block, axis, route)


def unpack(packed):
    offsets = jnp.arange(32, dtype=jnp.int32)
    bit_values = jnp.right_shift(packed[..., None], offsets) & 1
    return bit_values.reshape(packed.shape[:-1] + (packed.shape[-1] * 32,)).astype(jnp.float32)


def shards(
    xtiles, row_bits, col_bits, tile_row, tile_col, tile_count, user_panel, item_panel, test_panel
):
    tile_size, rank_width = item_panel.shape
    sketch_width = test_panel.shape[1]
    blocks = user_panel.shape[0] // tile_size
    slots = xtiles.shape[1]
    cycle_size = lax.axis_size("item")
    item_pos = lax.axis_index("item")
    user_size = lax.axis_size("user")
    joined = jnp.concatenate([item_panel, test_panel], axis=1)
    padded = padded_2(joined, (("item", 0),), tile_size)
    neighbours = padded.reshape(3, tile_size, rank_width + sketch_width)
    row_ids = tile_row[0]
    window = (tile_col[0] - item_pos + 1 + cycle_size) % cycle_size
    user_blocks = user_panel.reshape(blocks, tile_size, rank_width)
    tile_data = xtiles[0]
    row_seen = unpack(row_bits[0])
    col_seen = unpack(col_bits[0])
    tile_live = tile_count[0, 0]
    live_slots = (jnp.arange(slots, dtype=jnp.int32) < tile_live).astype(jnp.float32)
    observed = row_seen[:, :, None] * col_seen[:, None, :] * live_slots[:, None, None]
    picked = neighbours[window]
    predicted = jnp.einsum(
        "tak,tbk->tab",
        user_blocks[row_ids],
        picked[:, :, :rank_width],
        preferred_element_type=jnp.float32,
    )
    residue = (observed * (tile_data.astype(jnp.float32) - predicted)).astype(jnp.bfloat16)
    sketch_tiles = jnp.einsum(
        "tab,tbs->tas", residue, picked[:, :, rank_width:], preferred_element_type=jnp.float32
    )
    row_onehot = (row_ids[:, None] == jnp.arange(blocks, dtype=jnp.int32)[None, :]).astype(
        jnp.float32
    )
    partial_rows = jnp.einsum(
        "tr,tas->ras", row_onehot, sketch_tiles, precision=lax.Precision.HIGHEST
    )
    summed = lax.psum(partial_rows.reshape(blocks * tile_size, sketch_width), "item")
    sketch_blocks = summed.astype(jnp.bfloat16).reshape(blocks, tile_size, sketch_width)
    column_tiles = jnp.einsum(
        "tab,tas->tbs", residue, sketch_blocks[row_ids], preferred_element_type=jnp.float32
    )
    side_onehot = (window[:, None] == jnp.arange(3, dtype=jnp.int32)[None, :]).astype(jnp.float32)
    partial_cols = jnp.einsum(
        "tw,tbs->wbs", side_onehot, column_tiles, precision=lax.Precision.HIGHEST
    )
    sketch_scale = 2.0 / math.sqrt(user_size * slots * tile_size)
    from_upper = shifted(partial_cols[0], "item", -1)
    from_lower = shifted(partial_cols[2], "item", 1)
    own_terms = partial_cols[1] + from_upper + from_lower
    column_sum = lax.psum_scatter(own_terms, "user", scatter_dimension=0, tiled=True)
    return (summed, (column_sum * sketch_scale)[None])


def solution(mesh):
    placed = (
        P("user", "item", None, None),
        P("user", "item", None),
        P("user", "item", None),
        P("user", "item"),
        P("user", "item"),
        P("user", "item"),
        P("user", None),
        P("item", None),
        P("item", None),
    )
    return jax.shard_map(
        shards,
        mesh=mesh,
        in_specs=placed,
        out_specs=(P("user", None), P("item", "user", None)),
        check_vma=False,
    )
```

profile of v0, /device:TPU:0, one launch (start us, length us, event | category | flops | bytes accessed | tf_op | source)
XLA Modules:
  0.0 165.4 jit_solution(12587420773225362628)
XLA Ops:
  7.2 0.0 copy-start
  7.2 0.0 all-reduce.2.cloned.1.call-start
  7.2 0.9 constant_dynamic-update-slice_fusion.1
  8.2 0.9 constant_dynamic-update-slice_fusion
  9.1 2.5 %collective-permute-start.1 = (bf16[256,512]{1,0:T(8,128)(2,1)S(1)}, bf16[256,512]{1,0:T(8,128)(2,1)S(1)}, u32[]{:S(2)}, u32[]{:S(2)}) collective-permute-start(bf16[256,512]{1,0:T(8,128)(2,1)S(1)} %constant_dynamic-update-slice_fusion), channel_id=1, source_target_pairs={{1,0},{2,1},{3,2},{0,3},{5,4},{6,5},{7,6},{4,7},{9,8},{10,9},{11,1... | collective-permute-start | bytes 786440 | tf_op jit(solution)/shard_map/ppermute | solution.py:17
  11.6 0.0 collective-permute-start
  12.2 0.7 fusion.22
  12.9 0.7 fusion.23
  13.6 0.1 shift_right_arithmetic.56
  13.6 0.8 copy.15
  14.4 0.8 copy.16
  15.2 0.1 shift_right_arithmetic.60
  15.2 0.1 shift_right_arithmetic.61
  15.3 0.1 shift_right_arithmetic.53
  15.4 0.1 shift_right_arithmetic.54
  15.5 0.0 copy-done
  15.5 2.6 %gather_fusion = bf16[24,256,256]{2,1,0:T(8,128)(2,1)} fusion(bf16[2,256,256]{2,1,0:T(8,128)(2,1)S(1)} %bitcast.46, s32[1024]{0:T(1024)S(1)} %get-tuple-element.8), kind=kCustom, calls=%fused_computation | custom fusion | bytes 6291552 | tf_op jit(solution)/shard_map/gather | solution.py:59
  18.1 0.1 collective-permute-done.1
  18.2 1.1 collective-permute-done
  19.3 0.1 pad_maximum_fusion
  19.3 4.4 %gather_fusion.1 = bf16[24,256,512]{2,1,0:T(8,128)(2,1)} fusion(bf16[3,256,512]{2,1,0:T(8,128)(2,1)S(1)} %bitcast.47, s32[1024]{0:T(1024)S(1)} %get-tuple-element.7), kind=kCustom, calls=%fused_computation.1 | custom fusion | bytes 12583008 | tf_op jit(solution)/shard_map/gather | solution.py:56
  23.7 5.4 %fusion.1 = bf16[24,256,256]{2,1,0:T(8,128)(2,1)S(1)} fusion(bf16[1,24,256,256]{3,2,1,0:T(8,128)(2,1)} %param.9, f32[24]{0:T(128)S(1)} %compare_convert_fusion, f32[24,256]{1,0:T(8,128)S(1)} %get-tuple-element.6, f32[24,256]{1,0:T(8,128)S(1)} %get-tuple-element.5, bf16[24,256,256]{2,1,0:T(8,128)(2,1)} %gather_fusion, bf16[24,256,512]{2,1,0:T(8,128)(2,1)} %gather_fusion.1), kind=kOutput, calls=%fused_computation.5 | convolution fusion | flops 814743552 | bytes 12632160 | tf_op jit(solution)/shard_map/tak,tbk->tab/dot_general | solution.py:57
  29.1 0.1 copy-done.1
  29.2 1.0 fusion.6
  30.2 0.6 copy-done.2
  30.9 0.0 copy-done.4
  30.9 5.6 %fusion.4 = f32[2,256,256]{2,0,1:T(2,128)S(1)} fusion(f32[24,256,256]{2,1,0:T(8,128)S(1)} %fusion.6, s32[24]{0:T(128)S(1)} %bitcast.54), kind=kOutput, calls=%fused_computation.8 | convolution fusion | flops 37748784 | bytes 6815840 | tf_op jit(solution)/shard_map/tr,tas->ras/dot_general | solution.py:70
  36.5 0.8 copy.17
  37.3 0.0 all-reduce.2.cloned.1.call-update
  37.4 0.2 reduce-scatter.2.cloned.1.call-start
  37.6 0.0 copy-done.5
  37.6 34.2 %all-reduce.2.cloned.1.call-done = f32[512,256]{1,0:T(8,128)} async-done(((f32[512,256]{1,0:T(8,128)}), f32[512,256]{1,0:T(8,128)}) %all-reduce.2.cloned.1.call-update) | async-done | bytes 524304 | tf_op jit(solution)/shard_map/psum | solution.py:73
  71.8 1.1 convert_element_type.41
  72.9 2.5 %gather_fusion.2 = bf16[24,256,256]{2,1,0:T(8,128)(2,1)} fusion(bf16[2,256,256]{2,1,0:T(8,128)(2,1)S(1)} %bitcast.48, s32[1024]{0:T(1024)S(1)} %get-tuple-element.8), kind=kCustom, calls=%fused_computation.2 | custom fusion | bytes 6291552 | tf_op jit(solution)/shard_map/gather | solution.py:76
  75.4 3.9 %fusion.26 = f32[24,256,256]{2,1,0:T(8,128)S(1)} fusion(bf16[24,256,256]{2,1,0:T(8,128)(2,1)} %copy-done.2, bf16[24,256,256]{2,1,0:T(8,128)(2,1)} %gather_fusion.2), kind=kOutput, calls=%fused_computation.49 | convolution fusion | flops 805306368 | bytes 12582912 | tf_op jit(solution)/shard_map/tab,tas->tbs/dot_general | solution.py:75
  79.3 5.6 %fusion.2 = f32[3,256,256]{2,0,1:T(4,128)S(1)} fusion(f32[24,256,256]{2,1,0:T(8,128)S(1)} %fusion.26, s32[24]{0:T(128)S(1)} %and_select_fusion), kind=kOutput, calls=%fused_computation.6 | convolution fusion | flops 56623176 | bytes 7077984 | tf_op jit(solution)/shard_map/tw,tbs->wbs/dot_general | solution.py:79
  84.9 0.0 copy-start.3
  85.0 0.5 fusion.25
  85.6 0.1 collective-permute-start.2
  85.6 0.5 collective-permute-start.3
  86.1 6.0 %collective-permute-done.2 = f32[256,256]{1,0:T(8,128)S(1)} collective-permute-done((f32[256,256]{1,0:T(8,128)S(1)}, f32[256,256]{1,0:T(8,128)S(1)}, u32[]{:S(2)}, u32[]{:S(2)}) %collective-permute-start.2) | collective-permute-done | bytes 262176 | tf_op jit(solution)/shard_map/ppermute | solution.py:25
  92.1 0.8 collective-permute-done.3
  92.9 0.8 fusion.13
  93.6 0.0 reduce-scatter.2.cloned.1.call-update
  93.7 62.7 %reduce-scatter.2.cloned.1.call-done = f32[32,256]{1,0:T(8,128)} async-done(((f32[256,256]{1,0:T(8,128)}), f32[32,256]{1,0:T(8,128)}) %reduce-scatter.2.cloned.1.call-update) | async-done | bytes 32784 | tf_op jit(solution)/shard_map/reduce_scatter | solution.py:86
  156.4 1.4 multiply_bitcast_fusion
  157.8 0.0 copy-done.3
  157.8 0.8 copy.41
  (11 shorter events, 0.1 us)
Async XLA Ops:
  7.2 8.4 %copy-start = (bf16[512,256]{1,0:T(8,128)(2,1)S(1)}, bf16[512,256]{1,0:T(8,128)(2,1)}, u32[]{:S(2)}) copy-start(bf16[512,256]{1,0:T(8,128)(2,1)} %param.15) | copy-start | bytes 786436
  7.2 64.7 %all-reduce.2.cloned.1.call-start = ((), (), s32[]{:S(2)}) async-start(), calls=%async_computation.1 | async-start | bytes 1048576 | tf_op jit(solution)/shard_map/psum | solution.py:73
  9.1 9.1 %collective-permute-start.1 = (bf16[256,512]{1,0:T(8,128)(2,1)S(1)}, bf16[256,512]{1,0:T(8,128)(2,1)S(1)}, u32[]{:S(2)}, u32[]{:S(2)}) collective-permute-start(bf16[256,512]{1,0:T(8,128)(2,1)S(1)} %constant_dynamic-update-slice_fusion), channel_id=1, source_target_pairs={{1,0},{2,1},{3,2},{0,3},{5,4},{6,5},{7,6},{4,7},{9,8},{10,9},{11,1... | collective-permute-start | bytes 786440 | tf_op jit(solution)/shard_map/ppermute | solution.py:17
  11.6 7.7 %collective-permute-start = (bf16[256,512]{1,0:T(8,128)(2,1)S(1)}, bf16[256,512]{1,0:T(8,128)(2,1)S(1)}, u32[]{:S(2)}, u32[]{:S(2)}) collective-permute-start(bf16[256,512]{1,0:T(8,128)(2,1)S(1)} %constant_dynamic-update-slice_fusion), channel_id=1, source_target_pairs={{0,1},{1,2},{2,3},{3,0},{4,5},{5,6},{6,7},{7,4},{8,9},{9,10},{10,1... | collective-permute-start | bytes 786440 | tf_op jit(solution)/shard_map/ppermute | solution.py:16
  23.7 5.5 %copy-start.1 = (bf16[24,256,512]{2,1,0:T(8,128)(2,1)S(1)}, bf16[24,256,512]{2,1,0:T(8,128)(2,1)}, u32[]{:S(2)}) copy-start(bf16[24,256,512]{2,1,0:T(8,128)(2,1)} %gather_fusion.1) | copy-start | bytes 18874372
  29.2 1.6 copy-start.2
  29.2 1.6 copy-start.4
  30.9 6.7 %copy-start.5 = (s32[1,24]{1,0:T(1,128)S(1)}, s32[1,24]{1,0:T(1,128)}, u32[]{:S(2)}) copy-start(s32[1,24]{1,0:T(1,128)} %param.13) | copy-start | bytes 292
  37.4 119.0 %reduce-scatter.2.cloned.1.call-start = ((), (), s32[]{:S(2)}) async-start(), calls=%async_computation.2 | async-start | bytes 294912 | tf_op jit(solution)/shard_map/reduce_scatter | solution.py:86
  84.9 72.8 %copy-start.3 = (f32[512,256]{1,0:T(8,128)S(1)}, f32[512,256]{1,0:T(8,128)}, u32[]{:S(2)}) copy-start(f32[512,256]{1,0:T(8,128)} %all-reduce.2.cloned.1.call-done) | copy-start | bytes 1572868
  85.6 6.6 %collective-permute-start.2 = (f32[256,256]{1,0:T(8,128)S(1)}, f32[256,256]{1,0:T(8,128)S(1)}, u32[]{:S(2)}, u32[]{:S(2)}) collective-permute-start(f32[256,256]{1,0:T(8,128)S(1)} %bitcast.51), channel_id=1, source_target_pairs={{1,0},{2,1},{3,2},{0,3},{5,4},{6,5},{7,6},{4,7},{9,8},{10,9},{11,1... | collective-permute-start | bytes 786440 | tf_op jit(solution)/shard_map/ppermute | solution.py:25
  85.6 7.3 %collective-permute-start.3 = (f32[256,256]{1,0:T(8,128)S(1)}, f32[256,256]{1,0:T(8,128)S(1)}, u32[]{:S(2)}, u32[]{:S(2)}) collective-permute-start(f32[256,256]{1,0:T(8,128)S(1)} %bitcast.50), channel_id=1, source_target_pairs={{3,0},{0,1},{1,2},{2,3},{7,4},{4,5},{5,6},{6,7},{11,8},{8,9},{9,10... | collective-permute-start | bytes 786440 | tf_op jit(solution)/shard_map/ppermute | solution.py:25
Sparse Core Ops, SparseCore 0:
  37.5 34.3 all-reduce.1
  93.8 62.5 reduce-scatter.1
where the time goes:
time: 166 us; the launch traced here: 165 us
  waiting for transfers between devices  105 us (63%)
  matrix products  21.5 us (13%)
  local copies, waits for them, and re-layouts  16.2 us (10%)
  between operations  14.9 us (9%)
  other arithmetic  4.61 us (3%)
  starting transfers between devices  3.28 us (2%)
    reduce_scatter x1, waiting for transfers between devices, shards(): lax.psum_scatter(own_terms, 'user', scatter_dimension=0, tiled=True)  62.7 us
    psum x1, waiting for transfers between devices, shards(): lax.psum(partial_rows.reshape(blocks * tile_size, sketch_width), 'item')  34.2 us
    ppermute x2, waiting for transfers between devices, shifted(): return lax.ppermute(block, axis, route)  6.77 us
    dot_general x1, matrix products, shards(): jnp.einsum('tw,tbs->wbs', side_onehot, column_tiles, precision=lax.Precis...  5.63 us
    dot_general x1, matrix products, shards(): jnp.einsum('tr,tas->ras', row_onehot, sketch_tiles, precision=lax.Precisi...  5.63 us
    dot_general x1, matrix products, shards(): jnp.einsum('tak,tbk->tab', user_blocks[row_ids], picked[:, :, :rank_width...  5.43 us
    gather x1, local copies, waits for them, and re-layouts, shards(): picked = neighbours[window]  4.35 us
    dot_general x1, matrix products, shards(): jnp.einsum('tab,tas->tbs', residue, sketch_blocks[row_ids], preferred_ele...  3.88 us
  transfers between devices with their start and end apart: 6, of which 6 were waited for; matrix products, arithmetic and copies ran while one was open for 4% of the time, Pallas kernels for 0%

commit v1 on v0

v1 whole, which is shorter than its diff:
```python
import functools
import math

import jax
import jax.numpy as jnp
from jax import lax
from jax.experimental import pallas as pl
from jax.experimental.pallas import tpu as pltpu
from jax.sharding import PartitionSpec as P

MESH = pl.DeviceIdType.MESH
F32 = jnp.float32
BF16 = jnp.bfloat16
CHUNKS = 4


def sorting_pairs(length):
    size = 1 << (length - 1).bit_length()
    pairs = []
    p = 1
    while p < size:
        k = p
        while k >= 1:
            for j in range(k % p, size - k, 2 * k):
                for i in range(min(k, size - j - k)):
                    if (i + j) // (2 * p) == (i + j + k) // (2 * p):
                        pairs.append((i + j, i + j + k))
            k //= 2
        p *= 2
    return [(a, b) for a, b in pairs if b < length]


def kernel(
    n_user,
    n_item,
    scale,
    row_bits,
    col_bits,
    tile_row,
    tile_col,
    tile_count,
    user_ref,
    x_hbm,
    item_hbm,
    test_hbm,
    sketch_out,
    second_out,
    x_buf,
    v_all,
    t_all,
    p_buf,
    prefix,
    keys,
    a_hi,
    a_lo,
    at_hi,
    at_lo,
    half_send,
    half_recv,
    own_half,
    gathered,
    y_full,
    z_send,
    z_recv,
    z_own,
    piece_own,
    piece_send,
    piece_recv,
    local_sem,
    panel_send_sem,
    panel_recv_sem,
    half_send_sem,
    half_recv_sem,
    chip_send_sem,
    chip_recv_sem,
    y_send_sem,
    y_recv_sem,
    z_send_sem,
    z_recv_sem,
    piece_send_sem,
    piece_recv_sem,
):
    user = lax.axis_index("user")
    item = lax.axis_index("item")
    core = lax.rem(item, 2)
    chip = item // 2
    chips = n_item // 2
    slots, size = x_buf.shape[0], x_buf.shape[1]
    blocks = user_ref.shape[0] // size
    lower = lax.rem(item + n_item - 1, n_item)
    upper = lax.rem(item + 1, n_item)
    partner = chip * 2 + 1 - core
    far_window = 2 * core
    near_window = 2 - far_window
    far_item = jnp.where(core == 0, lower, upper)

    x_copy = pltpu.make_async_copy(x_hbm.at[0], x_buf, local_sem.at[0])
    v_copy = pltpu.make_async_copy(item_hbm, v_all.at[1], local_sem.at[1])
    t_copy = pltpu.make_async_copy(test_hbm, t_all.at[1], local_sem.at[2])
    v_copy.start()
    x_copy.start()
    t_copy.start()

    barrier = pltpu.get_barrier_semaphore()
    pl.semaphore_signal(barrier, inc=1, device_id={"item": far_item}, device_id_type=MESH)
    pl.semaphore_signal(barrier, inc=1, device_id={"item": partner}, device_id_type=MESH)
    for d in range(1, chips):
        other = lax.rem(chip + d, chips) * 2 + core
        pl.semaphore_signal(barrier, inc=1, device_id={"item": other}, device_id_type=MESH)
    for d in range(1, n_user):
        pl.semaphore_signal(
            barrier, inc=1, device_id={"user": lax.rem(user + d, n_user)}, device_id_type=MESH
        )
    pl.semaphore_wait(barrier, 2 + (chips - 1) + (n_user - 1))

    panel_copies = []
    for which, (source, target) in enumerate(((item_hbm, v_all), (test_hbm, t_all))):
        for side, (window, device) in enumerate(((near_window, far_item), (far_window, partner))):
            panel_copies.append(
                pltpu.make_async_remote_copy(
                    src_ref=source,
                    dst_ref=target.at[window],
                    send_sem=panel_send_sem.at[which, side],
                    recv_sem=panel_recv_sem.at[which, side],
                    device_id={"item": device},
                    device_id_type=MESH,
                )
            )
            panel_copies[-1].start()

    stride = 1 << (slots - 1).bit_length()
    order = []
    for t in range(slots):
        window = lax.rem(tile_col[0, t] - item + 1 + n_item, n_item)
        order.append((tile_row[0, t] * 3 + window) * stride + t)
    for a, b in sorting_pairs(slots):
        order[a], order[b] = jnp.minimum(order[a], order[b]), jnp.maximum(order[a], order[b])
    for t in range(slots):
        keys[t] = order[t]
    bounds = []
    for group in range(blocks * 3 + 1):
        bounds.append(sum((key < group * stride).astype(jnp.int32) for key in order))

    def predict(window):
        product = lax.dot_general(
            user_ref[...], v_all[window], (((1,), (1,)), ((), ())), preferred_element_type=F32
        )
        for r in range(blocks):
            p_buf[r * 3 + window] = product[r * size : (r + 1) * size]

    v_copy.wait()
    predict(1)
    prefix[0] = jnp.zeros((size, size), F32)
    panel_copies[1].wait_recv()
    panel_copies[0].wait_recv()
    predict(0)
    predict(2)
    x_copy.wait()

    strip = 16
    lanes = lax.broadcasted_iota(jnp.int32, (strip, size), 1)
    rows = lax.broadcasted_iota(jnp.int32, (strip, size), 0)

    def add_tile(i, carry):
        key = keys[i]
        t = jnp.bitwise_and(key, stride - 1)
        group = lax.shift_right_logical(key, stride.bit_length() - 1)
        live = (t < tile_count[0, 0]).astype(jnp.int32)
        words = jnp.zeros((strip, size), jnp.int32)
        for w in range(size // 32):
            words = jnp.where(lanes // 32 == w, col_bits[0, t, w] * live, words)
        col_seen = jnp.bitwise_and(lax.shift_right_logical(words, jnp.bitwise_and(lanes, 31)), 1)
        for s in range(size // strip):
            at = slice(s * strip, (s + 1) * strip)
            word = jnp.full((strip, size), row_bits[0, t, s * strip // 32], jnp.int32)
            seen = jnp.bitwise_and(
                lax.shift_right_logical(word, rows + (s * strip) % 32), col_seen
            )
            gap = x_buf[t, at, :].astype(F32) - p_buf[group, at, :]
            residue = jnp.where(seen != 0, gap, 0.0).astype(BF16)
            prefix[i + 1, at, :] = prefix[i, at, :] + residue.astype(F32)
        return carry

    lax.fori_loop(0, slots, add_tile, 0)

    for r in range(blocks):
        for window in range(3):
            group = r * 3 + window
            total = prefix[bounds[group + 1]] - prefix[bounds[group]]
            high = total.astype(BF16)
            a_hi[r, window] = high
            a_lo[r, window] = (total - high.astype(F32)).astype(BF16)
    t_copy.wait()
    panel_copies[3].wait_recv()
    panel_copies[2].wait_recv()

    def sketch_block(r):
        total = None
        for window in range(3):
            for part in (a_hi, a_lo):
                term = jnp.dot(part[r, window], t_all[window], preferred_element_type=F32)
                total = term if total is None else total + term
        return total

    step = size // CHUNKS
    half_send[...] = sketch_block(1 - core)
    half_copies = []
    for j in range(CHUNKS):
        at = pl.ds(j * step, step)
        half_copies.append(
            pltpu.make_async_remote_copy(
                src_ref=half_send.at[at],
                dst_ref=half_recv.at[at],
                send_sem=half_send_sem.at[j],
                recv_sem=half_recv_sem.at[j],
                device_id={"item": partner},
                device_id_type=MESH,
            )
        )
        half_copies[-1].start()
    own_half[...] = sketch_block(core)

    chip_copies = []
    for j in range(CHUNKS):
        at = pl.ds(j * step, step)
        half_copies[j].wait_recv()
        gathered[chip, at, :] = own_half[at, :] + half_recv[at, :]
        for d in range(1, chips):
            chip_copies.append(
                pltpu.make_async_remote_copy(
                    src_ref=gathered.at[chip, at],
                    dst_ref=gathered.at[chip, at],
                    send_sem=chip_send_sem.at[j, d - 1],
                    recv_sem=chip_recv_sem.at[j, d - 1],
                    device_id={"item": lax.rem(chip + d, chips) * 2 + core},
                    device_id_type=MESH,
                )
            )
            chip_copies[-1].start()

    for r in range(blocks):
        for window in range(3):
            group = r * 3 + window
            turned = (prefix[bounds[group + 1]] - prefix[bounds[group]]).T
            high = turned.astype(BF16)
            at_hi[window, :, r * size : (r + 1) * size] = high
            at_lo[window, :, r * size : (r + 1) * size] = (turned - high.astype(F32)).astype(BF16)

    y_copies = []
    for j in range(CHUNKS):
        at = pl.ds(j * step, step)
        for d in range(1, chips):
            chip_copies[j * (chips - 1) + d - 1].wait_recv()
        total = gathered[0, at, :]
        for other in range(1, chips):
            total = total + gathered[other, at, :]
        y_full[core, at, :] = total
        y_copies.append(
            pltpu.make_async_remote_copy(
                src_ref=y_full.at[core, at],
                dst_ref=y_full.at[core, at],
                send_sem=y_send_sem.at[j],
                recv_sem=y_recv_sem.at[j],
                device_id={"item": partner},
                device_id_type=MESH,
            )
        )
        y_copies[-1].start()
    for j in range(CHUNKS):
        y_copies[j].wait_recv()
    out_copy = pltpu.make_async_copy(y_full, sketch_out, local_sem.at[3])
    out_copy.start()
    y_half = y_full[...].astype(BF16).reshape(blocks * size, size)

    def second(window):
        return jnp.dot(at_hi[window], y_half, preferred_element_type=F32) + jnp.dot(
            at_lo[window], y_half, preferred_element_type=F32
        )

    piece = size // n_user
    turns = sorted(range(1, n_user), key=lambda d: -min(d, n_user - d)) + [0]
    z_copies = [[], []]
    for side, (window, facing, device) in enumerate(
        ((far_window, near_window, far_item), (near_window, far_window, partner))
    ):
        z_send[side] = second(window).astype(z_send.dtype).reshape(n_user, piece, size)
        for n, d in enumerate(turns):
            target = lax.rem(user + d, n_user)
            z_copies[side].append(
                pltpu.make_async_remote_copy(
                    src_ref=z_send.at[side, target],
                    dst_ref=z_recv.at[side, target],
                    send_sem=z_send_sem.at[side, n],
                    recv_sem=z_recv_sem.at[side, n],
                    device_id={"item": device},
                    device_id_type=MESH,
                )
            )
            z_copies[side][-1].start()
    z_own[...] = second(1).reshape(n_user, piece, size)

    piece_copies = []
    for n, d in enumerate(turns):
        target = lax.rem(user + d, n_user)
        z_copies[1][n].wait_recv()
        z_copies[0][n].wait_recv()
        total = z_own[target] + z_recv[0, target].astype(F32) + z_recv[1, target].astype(F32)
        if d == 0:
            piece_own[...] = total
            continue
        piece_send[target] = total.astype(piece_send.dtype)
        piece_copies.append(
            pltpu.make_async_remote_copy(
                src_ref=piece_send.at[target],
                dst_ref=piece_recv.at[n],
                send_sem=piece_send_sem.at[n],
                recv_sem=piece_recv_sem.at[n],
                device_id={"user": target},
                device_id_type=MESH,
            )
        )
        piece_copies[-1].start()
    total = piece_own[...]
    for n, copy in enumerate(piece_copies):
        copy.wait_recv()
        total = total + piece_recv[n].astype(F32)
    second_out[0] = total * scale

    out_copy.wait()
    for copy in panel_copies + half_copies + chip_copies + y_copies + z_copies[0] + z_copies[1]:
        copy.wait_send()
    for copy in piece_copies:
        copy.wait_send()


def shards(
    xtiles, row_bits, col_bits, tile_row, tile_col, tile_count, user_panel, item_panel, test_panel
):
    size = item_panel.shape[0]
    slots = xtiles.shape[1]
    blocks = user_panel.shape[0] // size
    n_user, n_item = lax.axis_size("user"), lax.axis_size("item")
    chips = n_item // 2
    piece = size // n_user
    sent = BF16 if piece % 16 == 0 else F32
    scale = 2.0 / math.sqrt(n_user * slots * size)
    square = (size, size)
    dma = pltpu.SemaphoreType.DMA
    smem = pl.BlockSpec(memory_space=pltpu.SMEM)
    vmem = pl.BlockSpec(memory_space=pltpu.VMEM)
    hbm = pl.BlockSpec(memory_space=pl.ANY)
    sketch, second = pl.pallas_call(
        functools.partial(kernel, n_user, n_item, scale),
        out_shape=(
            jax.ShapeDtypeStruct((blocks,) + square, F32),
            jax.ShapeDtypeStruct((1, piece, size), F32),
        ),
        in_specs=[smem] * 5 + [vmem] + [hbm] * 3,
        out_specs=(hbm, vmem),
        scratch_shapes=[
            pltpu.VMEM((slots,) + square, BF16),
            pltpu.VMEM((3,) + square, BF16),
            pltpu.VMEM((3,) + square, BF16),
            pltpu.VMEM((blocks * 3,) + square, F32),
            pltpu.VMEM((slots + 1,) + square, F32),
            pltpu.SMEM((slots,), jnp.int32),
            pltpu.VMEM((blocks, 3) + square, BF16),
            pltpu.VMEM((blocks, 3) + square, BF16),
            pltpu.VMEM((3, size, blocks * size), BF16),
            pltpu.VMEM((3, size, blocks * size), BF16),
            pltpu.VMEM(square, F32),
            pltpu.VMEM(square, F32),
            pltpu.VMEM(square, F32),
            pltpu.VMEM((chips,) + square, F32),
            pltpu.VMEM((blocks,) + square, F32),
            pltpu.VMEM((2, n_user, piece, size), sent),
            pltpu.VMEM((2, n_user, piece, size), sent),
            pltpu.VMEM((n_user, piece, size), F32),
            pltpu.VMEM((piece, size), F32),
            pltpu.VMEM((n_user, piece, size), sent),
            pltpu.VMEM((n_user - 1, piece, size), sent),
            dma((4,)),
            dma((2, 2)),
            dma((2, 2)),
            dma((CHUNKS,)),
            dma((CHUNKS,)),
            dma((CHUNKS, chips - 1)),
            dma((CHUNKS, chips - 1)),
            dma((CHUNKS,)),
            dma((CHUNKS,)),
            dma((2, n_user)),
            dma((2, n_user)),
            dma((n_user - 1,)),
            dma((n_user - 1,)),
        ],
        compiler_params=pltpu.CompilerParams(
            collective_id=0, has_side_effects=True, vmem_limit_bytes=48 * 1024 * 1024
        ),
    )(
        row_bits,
        col_bits,
        tile_row,
        tile_col,
        tile_count,
        user_panel,
        xtiles,
        item_panel,
        test_panel,
    )
    return sketch.reshape(blocks * size, size), second


def solution(mesh):
    placed = (
        P("user", "item", None, None),
        P("user", "item", None),
        P("user", "item", None),
        P("user", "item"),
        P("user", "item"),
        P("user", "item"),
        P("user", None),
        P("item", None),
        P("item", None),
    )
    return jax.shard_map(
        shards,
        mesh=mesh,
        in_specs=placed,
        out_specs=(P("user", None), P("item", "user", None)),
        check_vma=False,
    )
```

time: 166 us -> 44.1 us (0.27)
  waiting for transfers between devices: 105 us -> 0 us
  Pallas kernels: 0 us -> 33.6 us
  matrix products: 21.5 us -> 0 us
  between operations: 14.9 us -> 1.29 us
  local copies, waits for them, and re-layouts: 16.2 us -> 8.88 us
  other arithmetic: 4.61 us -> 0 us
  starting transfers between devices: 3.28 us -> 0 us
    reduce_scatter x1 -> x0, waiting for transfers between devices: 62.7 us -> none  [shards(): lax.psum_scatter(own_terms, 'user', scatter_dimension=0, tiled=True)]
    psum x1 -> x0, waiting for transfers between devices: 34.2 us -> none  [shards(): lax.psum(partial_rows.reshape(blocks * tile_size, sketch_width), 'item')]
    pallas_call x0 -> x1, Pallas kernels: none -> 33.6 us  [shards(): pl.pallas_call(functools.partial(kernel, n_user, n_item, scale), out_shap...]
    dot_general x5 -> x0, matrix products: 21.5 us -> none  [the longest x1 5.63 us: shards(): jnp.einsum('tw,tbs->wbs', side_onehot, column_tiles, precision=lax.Precis...]
    gather x3 -> x0, local copies, waits for them, and re-layouts: 9.44 us -> none  [the longest x1 4.35 us: shards(): picked = neighbours[window]]
    ppermute x4 -> x0, waiting for transfers between devices: 7.92 us -> none  [the longest x2 6.77 us: shifted(): return lax.ppermute(block, axis, route)]
    unnamed x16, local copies, waits for them, and re-layouts: 2.55 us -> 8.88 us
    ppermute x4 -> x0, starting transfers between devices: 3.02 us -> none  [the longest x1 2.46 us: padded_2(): after = lax.ppermute(first, axis, down)]
  transfers between devices with their start and end apart: 6 -> 0, of which waited for: 6 -> 0; matrix products, arithmetic and copies ran while one was open for 4% -> 0% of each run, Pallas kernels for 0% -> 0%
where the time goes in v1:
time: 44.1 us; the launch traced here: 43.8 us
  Pallas kernels  33.6 us (76%)
  local copies, waits for them, and re-layouts  8.88 us (20%)
  between operations  1.29 us (3%)
    pallas_call x1, Pallas kernels, shards(): pl.pallas_call(functools.partial(kernel, n_user, n_item, scale), out_shap...  33.6 us
    unnamed x16, local copies, waits for them, and re-layouts  8.88 us

profile of v1, /device:TPU:0, one launch (start us, length us, event | category | flops | bytes accessed | tf_op | source)
XLA Modules:
  0.0 43.8 jit_solution(17006607982102085799)
XLA Ops:
  1.3 0.8 %copy.11.row_bits = s32[1,24,8]{2,1,0:T(8,128)S(1)} copy(s32[1,24,8]{1,2,0:T(8,128)} %param.10) | data formatting | bytes 1536 | tf_op args[1]
  2.0 0.8 %copy.12.col_bits = s32[1,24,8]{2,1,0:T(8,128)S(1)} copy(s32[1,24,8]{1,2,0:T(8,128)} %param.11) | data formatting | bytes 1536 | tf_op args[2]
  2.8 0.0 copy-start
  2.8 1.9 %copy-done = bf16[1,24,256,256]{3,2,1,0:T(8,128)(2,1)S(1)} copy-done((bf16[1,24,256,256]{3,2,1,0:T(8,128)(2,1)S(1)}, bf16[1,24,256,256]{3,2,1,0:T(8,128)(2,1)}, u32[]{:S(2)}) %copy-start) | copy-done | bytes 3145752
  4.7 0.0 copy-start.1
  4.7 0.9 %copy-done.1 = bf16[512,256]{1,0:T(8,128)(2,1)S(1)} copy-done((bf16[512,256]{1,0:T(8,128)(2,1)S(1)}, bf16[512,256]{1,0:T(8,128)(2,1)}, u32[]{:S(2)}) %copy-start.1) | copy-done | bytes 262168
  5.6 0.0 copy-start.2
  5.6 0.9 %copy-done.2 = bf16[256,256]{1,0:T(8,128)(2,1)S(1)} copy-done((bf16[256,256]{1,0:T(8,128)(2,1)S(1)}, bf16[256,256]{1,0:T(8,128)(2,1)}, u32[]{:S(2)}) %copy-start.2) | copy-done | bytes 131096
  6.5 0.0 copy-start.3
  6.5 0.9 %copy-done.3 = bf16[256,256]{1,0:T(8,128)(2,1)S(1)} copy-done((bf16[256,256]{1,0:T(8,128)(2,1)S(1)}, bf16[256,256]{1,0:T(8,128)(2,1)}, u32[]{:S(2)}) %copy-start.3) | copy-done | bytes 131096
  7.4 0.0 copy-start.4
  7.4 0.7 %copy-done.4 = s32[1,24]{1,0:T(1,128)S(1)} copy-done((s32[1,24]{1,0:T(1,128)S(1)}, s32[1,24]{1,0:T(1,128)}, u32[]{:S(2)}) %copy-start.4) | copy-done | bytes 120
  8.1 0.0 copy-start.5
  8.1 0.7 %copy-done.5 = s32[1,24]{1,0:T(1,128)S(1)} copy-done((s32[1,24]{1,0:T(1,128)S(1)}, s32[1,24]{1,0:T(1,128)}, u32[]{:S(2)}) %copy-start.5) | copy-done | bytes 120
  8.8 33.6 %shard_map.104 = (f32[2,256,256]{2,1,0:T(8,128)S(1)}, f32[1,32,256]{2,1,0:T(8,128)S(1)}) custom-call(s32[1,24,8]{2,1,0:T(8,128)S(1)} %copy.11.row_bits, s32[1,24,8]{2,1,0:T(8,128)S(1)} %copy.12.col_bits, s32[1,24]{1,0:T(1,128)S(1)} %copy-done.4, s32[1,24]{1,0:T(1,128)S(1)} %copy-done.5, s32[1,1]{1,0:T(1,128)S(6)} %copy.15.tile_count, ...), custom_call_target="tpu_custom_call" | custom-call | tf_op jit(solution)/shard_map/pallas_call | solution.py:352
  42.4 0.8 %copy.16 = f32[512,256]{1,0:T(8,128)} copy(f32[512,256]{1,0:T(8,128)S(1)} %bitcast.1) | data formatting | bytes 1048576
  43.2 0.6 %copy.17 = f32[1,32,256]{2,1,0:T(8,128)} copy(f32[1,32,256]{2,1,0:T(8,128)S(1)} %get-tuple-element.9) | data formatting | bytes 65536
Async XLA Ops:
  2.8 1.9 %copy-start = (bf16[1,24,256,256]{3,2,1,0:T(8,128)(2,1)S(1)}, bf16[1,24,256,256]{3,2,1,0:T(8,128)(2,1)}, u32[]{:S(2)}) copy-start(bf16[1,24,256,256]{3,2,1,0:T(8,128)(2,1)} %x_hbm.1) | copy-start | bytes 9437188
  4.7 0.9 %copy-start.1 = (bf16[512,256]{1,0:T(8,128)(2,1)S(1)}, bf16[512,256]{1,0:T(8,128)(2,1)}, u32[]{:S(2)}) copy-start(bf16[512,256]{1,0:T(8,128)(2,1)} %user_ref.1) | copy-start | bytes 786436
  5.6 0.9 %copy-start.2 = (bf16[256,256]{1,0:T(8,128)(2,1)S(1)}, bf16[256,256]{1,0:T(8,128)(2,1)}, u32[]{:S(2)}) copy-start(bf16[256,256]{1,0:T(8,128)(2,1)} %item_hbm.1) | copy-start | bytes 393220
  6.5 0.9 %copy-start.3 = (bf16[256,256]{1,0:T(8,128)(2,1)S(1)}, bf16[256,256]{1,0:T(8,128)(2,1)}, u32[]{:S(2)}) copy-start(bf16[256,256]{1,0:T(8,128)(2,1)} %test_hbm.1) | copy-start | bytes 393220
  7.4 0.7 %copy-start.4 = (s32[1,24]{1,0:T(1,128)S(1)}, s32[1,24]{1,0:T(1,128)}, u32[]{:S(2)}) copy-start(s32[1,24]{1,0:T(1,128)} %tile_row.1) | copy-start | bytes 292
  8.1 0.7 %copy-start.5 = (s32[1,24]{1,0:T(1,128)S(1)}, s32[1,24]{1,0:T(1,128)}, u32[]{:S(2)}) copy-start(s32[1,24]{1,0:T(1,128)} %tile_col.1) | copy-start | bytes 292

commit v2 on v1

--- a/solution.py
+++ b/solution.py
@@ -34,18 +34,25 @@
     n_user,
     n_item,
     scale,
+    row_bits_hbm,
+    col_bits_hbm,
+    tile_row_hbm,
+    tile_col_hbm,
+    tile_count_hbm,
+    user_hbm,
+    x_hbm,
+    item_hbm,
+    test_hbm,
+    sketch_out,
+    second_out,
     row_bits,
     col_bits,
     tile_row,
     tile_col,
     tile_count,
     user_ref,
-    x_hbm,
-    item_hbm,
-    test_hbm,
-    sketch_out,
-    second_out,
     x_buf,
+    masks,
     v_all,
     t_all,
     p_buf,
@@ -97,9 +104,21 @@
     x_copy = pltpu.make_async_copy(x_hbm.at[0], x_buf, local_sem.at[0])
     v_copy = pltpu.make_async_copy(item_hbm, v_all.at[1], local_sem.at[1])
     t_copy = pltpu.make_async_copy(test_hbm, t_all.at[1], local_sem.at[2])
-    v_copy.start()
-    x_copy.start()
-    t_copy.start()
+    u_copy = pltpu.make_async_copy(user_hbm, user_ref, local_sem.at[4])
+    small_copies = [
+        pltpu.make_async_copy(source, target, local_sem.at[5 + n])
+        for n, (source, target) in enumerate(
+            (
+                (tile_row_hbm, tile_row),
+                (tile_col_hbm, tile_col),
+                (tile_count_hbm, tile_count),
+                (row_bits_hbm, row_bits),
+                (col_bits_hbm, col_bits),
+            )
+        )
+    ]
+    for copy in small_copies + [u_copy, v_copy, x_copy, t_copy]:
+        copy.start()
 
     barrier = pltpu.get_barrier_semaphore()
     pl.semaphore_signal(barrier, inc=1, device_id={"item": far_item}, device_id_type=MESH)
@@ -128,6 +147,28 @@
             )
             panel_copies[-1].start()
 
+    for copy in small_copies:
+        copy.wait()
+    strip = 16
+    lanes = lax.broadcasted_iota(jnp.int32, (strip, size), 1)
+    rows = lax.broadcasted_iota(jnp.int32, (strip, size), 0)
+
+    def make_mask(t, carry):
+        live = (t < tile_count[0, 0]).astype(jnp.int32)
+        words = jnp.zeros((strip, size), jnp.int32)
+        for w in range(size // 32):
+            words = jnp.where(lanes // 32 == w, col_bits[0, w, t] * live, words)
+        col_seen = jnp.bitwise_and(lax.shift_right_logical(words, jnp.bitwise_and(lanes, 31)), 1)
+        for s in range(size // strip):
+            word = jnp.full((strip, size), row_bits[0, s * strip // 32, t], jnp.int32)
+            seen = jnp.bitwise_and(
+                lax.shift_right_logical(word, rows + (s * strip) % 32), col_seen
+            )
+            masks[t, s * strip : (s + 1) * strip, :] = seen.astype(F32).astype(BF16)
+        return carry
+
+    lax.fori_loop(0, slots, make_mask, 0)
+
     stride = 1 << (slots - 1).bit_length()
     order = []
     for t in range(slots):
@@ -148,36 +189,24 @@
         for r in range(blocks):
             p_buf[r * 3 + window] = product[r * size : (r + 1) * size]
 
+    prefix[0] = jnp.zeros((size, size), F32)
+    u_copy.wait()
     v_copy.wait()
     predict(1)
-    prefix[0] = jnp.zeros((size, size), F32)
     panel_copies[1].wait_recv()
+    predict(near_window)
+    x_copy.wait()
     panel_copies[0].wait_recv()
-    predict(0)
-    predict(2)
-    x_copy.wait()
-
-    strip = 16
-    lanes = lax.broadcasted_iota(jnp.int32, (strip, size), 1)
-    rows = lax.broadcasted_iota(jnp.int32, (strip, size), 0)
+    predict(far_window)
 
     def add_tile(i, carry):
         key = keys[i]
         t = jnp.bitwise_and(key, stride - 1)
         group = lax.shift_right_logical(key, stride.bit_length() - 1)
-        live = (t < tile_count[0, 0]).astype(jnp.int32)
-        words = jnp.zeros((strip, size), jnp.int32)
-        for w in range(size // 32):
-            words = jnp.where(lanes // 32 == w, col_bits[0, t, w] * live, words)
-        col_seen = jnp.bitwise_and(lax.shift_right_logical(words, jnp.bitwise_and(lanes, 31)), 1)
         for s in range(size // strip):
             at = slice(s * strip, (s + 1) * strip)
-            word = jnp.full((strip, size), row_bits[0, t, s * strip // 32], jnp.int32)
-            seen = jnp.bitwise_and(
-                lax.shift_right_logical(word, rows + (s * strip) % 32), col_seen
-            )
             gap = x_buf[t, at, :].astype(F32) - p_buf[group, at, :]
-            residue = jnp.where(seen != 0, gap, 0.0).astype(BF16)
+            residue = gap.astype(BF16) * masks[t, at, :]
             prefix[i + 1, at, :] = prefix[i, at, :] + residue.astype(F32)
         return carry
 
@@ -333,6 +362,16 @@
         copy.wait_send()
 
 
+def hand_over(sketch, second, sketch_out, second_out, sem):
+    copies = [pltpu.make_async_copy(second, second_out, sem.at[0])]
+    for r in range(sketch.shape[0]):
+        copies.append(pltpu.make_async_copy(sketch.at[r], sketch_out.at[r], sem.at[1 + r]))
+    for copy in copies:
+        copy.start()
+    for copy in copies:
+        copy.wait()
+
+
 def shards(
     xtiles, row_bits, col_bits, tile_row, tile_col, tile_count, user_panel, item_panel, test_panel
 ):
@@ -345,19 +384,26 @@
     sent = BF16 if piece % 16 == 0 else F32
     scale = 2.0 / math.sqrt(n_user * slots * size)
     square = (size, size)
+    words = row_bits.shape[2]
     dma = pltpu.SemaphoreType.DMA
-    smem = pl.BlockSpec(memory_space=pltpu.SMEM)
     vmem = pl.BlockSpec(memory_space=pltpu.VMEM)
-    hbm = pl.BlockSpec(memory_space=pl.ANY)
+    hbm = pl.BlockSpec(memory_space=pltpu.HBM)
     sketch, second = pl.pallas_call(
         functools.partial(kernel, n_user, n_item, scale),
         out_shape=(
             jax.ShapeDtypeStruct((blocks,) + square, F32),
             jax.ShapeDtypeStruct((1, piece, size), F32),
         ),
-        in_specs=[smem] * 5 + [vmem] + [hbm] * 3,
+        in_specs=[hbm] * 9,
         out_specs=(hbm, vmem),
         scratch_shapes=[
+            pltpu.SMEM((1, words, slots), jnp.int32),
+            pltpu.SMEM((1, words, slots), jnp.int32),
+            pltpu.SMEM((1, slots), jnp.int32),
+            pltpu.SMEM((1, slots), jnp.int32),
+            pltpu.SMEM((1, 1), jnp.int32),
+            pltpu.VMEM(user_panel.shape, BF16),
+            pltpu.VMEM((slots,) + square, BF16),
             pltpu.VMEM((slots,) + square, BF16),
             pltpu.VMEM((3,) + square, BF16),
             pltpu.VMEM((3,) + square, BF16),
@@ -379,7 +425,7 @@
             pltpu.VMEM((piece, size), F32),
             pltpu.VMEM((n_user, piece, size), sent),
             pltpu.VMEM((n_user - 1, piece, size), sent),
-            dma((4,)),
+            dma((10,)),
             dma((2, 2)),
             dma((2, 2)),
             dma((CHUNKS,)),
@@ -394,11 +440,11 @@
             dma((n_user - 1,)),
         ],
         compiler_params=pltpu.CompilerParams(
-            collective_id=0, has_side_effects=True, vmem_limit_bytes=48 * 1024 * 1024
+            collective_id=0, has_side_effects=True, vmem_limit_bytes=63 * 1024 * 1024
         ),
     )(
-        row_bits,
-        col_bits,
+        jnp.swapaxes(row_bits, 1, 2),
+        jnp.swapaxes(col_bits, 1, 2),
         tile_row,
         tile_col,
         tile_count,
@@ -407,6 +453,17 @@
         item_panel,
         test_panel,
     )
+    sketch, second = pl.pallas_call(
+        hand_over,
+        out_shape=(
+            jax.ShapeDtypeStruct(sketch.shape, F32),
+            jax.ShapeDtypeStruct(second.shape, F32),
+        ),
+        in_specs=[hbm] * 2,
+        out_specs=(hbm, hbm),
+        scratch_shapes=[dma((blocks + 1,))],
+        compiler_params=pltpu.CompilerParams(vmem_limit_bytes=63 * 1024 * 1024),
+    )(sketch, second)
     return sketch.reshape(blocks * size, size), second
 
 

time: 44.1 us -> 51.8 us (1.17)
  Pallas kernels: 33.6 us -> 50.4 us
  local copies, waits for them, and re-layouts: 8.88 us -> 0 us
    pallas_call x0 -> x1, Pallas kernels: none -> 18 us  [shards(): pl.pallas_call(hand_over, out_shape=(jax.ShapeDtypeStruct(sketch.shape, F...]
    unnamed x16 -> x0, local copies, waits for them, and re-layouts: 8.88 us -> none
    pallas_call x1, Pallas kernels: 33.6 us -> 32.4 us  [shards(): pl.pallas_call(functools.partial(kernel, n_user, n_item, scale), out_shap...]
where the time goes in v2:
time: 51.8 us; the launch traced here: 51.7 us
  Pallas kernels  50.4 us (97%)
  between operations  1.29 us (2%)
    pallas_call x1, Pallas kernels, shards(): pl.pallas_call(functools.partial(kernel, n_user, n_item, scale), out_shap...  32.4 us
    pallas_call x1, Pallas kernels, shards(): pl.pallas_call(hand_over, out_shape=(jax.ShapeDtypeStruct(sketch.shape, F...  18 us

profile of v2, /device:TPU:0, one launch (start us, length us, event | category | flops | bytes accessed | tf_op | source)
XLA Modules:
  0.0 51.7 jit_solution(1190729385678513113)
XLA Ops:
  1.3 32.4 %shard_map.104 = (f32[2,256,256]{2,1,0:T(8,128)}, f32[1,32,256]{2,1,0:T(8,128)}) custom-call(s32[1,8,24]{2,1,0:T(8,128)} %bitcast.3, s32[1,8,24]{2,1,0:T(8,128)} %bitcast.4, s32[1,24]{1,0:T(1,128)} %tile_row_hbm.1, s32[1,24]{1,0:T(1,128)} %tile_col_hbm.1, s32[1,1]{1,0:T(1,128)S(6)} %copy.11.tile_count_hbm, bf16[512,256]{1,0:T(8,128)(2,1)} %user_hbm.1, ...), custom_call_target="tpu_custom_call" | custom-call | tf_op jit(solution)/shard_map/pallas_call | solution.py:391
  33.7 18.0 %shard_map.105 = (f32[2,256,256]{2,1,0:T(8,128)}, f32[1,32,256]{2,1,0:T(8,128)}) custom-call(f32[2,256,256]{2,1,0:T(8,128)} %get-tuple-element.6.sketch, f32[1,32,256]{2,1,0:T(8,128)} %get-tuple-element.7.second), custom_call_target="tpu_custom_call" | custom-call | tf_op jit(solution)/shard_map/pallas_call | solution.py:456

commit v3 on v2

--- a/solution.py
+++ b/solution.py
@@ -58,6 +58,7 @@
     p_buf,
     prefix,
     keys,
+    bounds,
     a_hi,
     a_lo,
     at_hi,
@@ -67,8 +68,11 @@
     own_half,
     gathered,
     y_full,
-    z_send,
-    z_recv,
+    z_part,
+    far_send,
+    far_recv,
+    near_send,
+    near_recv,
     z_own,
     piece_own,
     piece_send,
@@ -178,9 +182,8 @@
         order[a], order[b] = jnp.minimum(order[a], order[b]), jnp.maximum(order[a], order[b])
     for t in range(slots):
         keys[t] = order[t]
-    bounds = []
     for group in range(blocks * 3 + 1):
-        bounds.append(sum((key < group * stride).astype(jnp.int32) for key in order))
+        bounds[group] = sum((key < group * stride).astype(jnp.int32) for key in order)
 
     def predict(window):
         product = lax.dot_general(
@@ -212,13 +215,18 @@
 
     lax.fori_loop(0, slots, add_tile, 0)
 
-    for r in range(blocks):
+    def group_sum(r, window):
+        group = r * 3 + window
+        return prefix[bounds[group + 1]] - prefix[bounds[group]]
+
+    def split_sums(r):
         for window in range(3):
-            group = r * 3 + window
-            total = prefix[bounds[group + 1]] - prefix[bounds[group]]
+            total = group_sum(r, window)
             high = total.astype(BF16)
             a_hi[r, window] = high
             a_lo[r, window] = (total - high.astype(F32)).astype(BF16)
+
+    split_sums(1 - core)
     t_copy.wait()
     panel_copies[3].wait_recv()
     panel_copies[2].wait_recv()
@@ -247,13 +255,14 @@
             )
         )
         half_copies[-1].start()
+    split_sums(core)
     own_half[...] = sketch_block(core)
 
     chip_copies = []
     for j in range(CHUNKS):
         at = pl.ds(j * step, step)
         half_copies[j].wait_recv()
-        gathered[chip, at, :] = own_half[at, :] + half_recv[at, :]
+        gathered[chip, at, :] = (own_half[at, :] + half_recv[at, :]).astype(BF16)
         for d in range(1, chips):
             chip_copies.append(
                 pltpu.make_async_remote_copy(
@@ -269,20 +278,19 @@
 
     for r in range(blocks):
         for window in range(3):
-            group = r * 3 + window
-            turned = (prefix[bounds[group + 1]] - prefix[bounds[group]]).T
+            turned = group_sum(r, window).T
             high = turned.astype(BF16)
-            at_hi[window, :, r * size : (r + 1) * size] = high
-            at_lo[window, :, r * size : (r + 1) * size] = (turned - high.astype(F32)).astype(BF16)
+            at_hi[r, window] = high
+            at_lo[r, window] = (turned - high.astype(F32)).astype(BF16)
 
     y_copies = []
     for j in range(CHUNKS):
         at = pl.ds(j * step, step)
         for d in range(1, chips):
             chip_copies[j * (chips - 1) + d - 1].wait_recv()
-        total = gathered[0, at, :]
+        total = gathered[0, at, :].astype(F32)
         for other in range(1, chips):
-            total = total + gathered[other, at, :]
+            total = total + gathered[other, at, :].astype(F32)
         y_full[core, at, :] = total
         y_copies.append(
             pltpu.make_async_remote_copy(
@@ -295,30 +303,36 @@
             )
         )
         y_copies[-1].start()
+    def second(r, window, y_half):
+        return jnp.dot(at_hi[r, window], y_half, preferred_element_type=F32) + jnp.dot(
+            at_lo[r, window], y_half, preferred_element_type=F32
+        )
+
+    y_half = y_full[core].astype(BF16)
+    for window in range(3):
+        z_part[window] = second(core, window, y_half)
     for j in range(CHUNKS):
         y_copies[j].wait_recv()
     out_copy = pltpu.make_async_copy(y_full, sketch_out, local_sem.at[3])
     out_copy.start()
-    y_half = y_full[...].astype(BF16).reshape(blocks * size, size)
-
-    def second(window):
-        return jnp.dot(at_hi[window], y_half, preferred_element_type=F32) + jnp.dot(
-            at_lo[window], y_half, preferred_element_type=F32
-        )
+    y_half = y_full[1 - core].astype(BF16)
+
+    def term(window):
+        return (z_part[window] + second(1 - core, window, y_half)).reshape(n_user, piece, size)
 
     piece = size // n_user
     turns = sorted(range(1, n_user), key=lambda d: -min(d, n_user - d)) + [0]
     z_copies = [[], []]
-    for side, (window, facing, device) in enumerate(
-        ((far_window, near_window, far_item), (near_window, far_window, partner))
+    for side, (window, device, z_send, z_recv) in enumerate(
+        ((far_window, far_item, far_send, far_recv), (near_window, partner, near_send, near_recv))
     ):
-        z_send[side] = second(window).astype(z_send.dtype).reshape(n_user, piece, size)
+        z_send[...] = term(window).astype(z_send.dtype)
         for n, d in enumerate(turns):
             target = lax.rem(user + d, n_user)
             z_copies[side].append(
                 pltpu.make_async_remote_copy(
-                    src_ref=z_send.at[side, target],
-                    dst_ref=z_recv.at[side, target],
+                    src_ref=z_send.at[target],
+                    dst_ref=z_recv.at[target],
                     send_sem=z_send_sem.at[side, n],
                     recv_sem=z_recv_sem.at[side, n],
                     device_id={"item": device},
@@ -326,14 +340,14 @@
                 )
             )
             z_copies[side][-1].start()
-    z_own[...] = second(1).reshape(n_user, piece, size)
+    z_own[...] = term(1)
 
     piece_copies = []
     for n, d in enumerate(turns):
         target = lax.rem(user + d, n_user)
         z_copies[1][n].wait_recv()
         z_copies[0][n].wait_recv()
-        total = z_own[target] + z_recv[0, target].astype(F32) + z_recv[1, target].astype(F32)
+        total = z_own[target] + near_recv[target] + far_recv[target].astype(F32)
         if d == 0:
             piece_own[...] = total
             continue
@@ -362,14 +376,23 @@
         copy.wait_send()
 
 
-def hand_over(sketch, second, sketch_out, second_out, sem):
-    copies = [pltpu.make_async_copy(second, second_out, sem.at[0])]
+def hand_over(sketch, second, sketch_out, second_out, sketch_buf, second_buf, sem):
+    triples = [(second, second_buf, second_out)]
+    half = sketch.shape[1] // 2
     for r in range(sketch.shape[0]):
-        copies.append(pltpu.make_async_copy(sketch.at[r], sketch_out.at[r], sem.at[1 + r]))
-    for copy in copies:
-        copy.start()
-    for copy in copies:
-        copy.wait()
+        for h in range(2):
+            at = pl.ds(h * half, half)
+            triples.append((sketch.at[r, at], sketch_buf.at[r, at], sketch_out.at[r, at]))
+    reads, writes = [], []
+    for n, (source, buffer, target) in enumerate(triples):
+        reads.append(pltpu.make_async_copy(source, buffer, sem.at[0, n]))
+        writes.append(pltpu.make_async_copy(buffer, target, sem.at[1, n]))
+        reads[-1].start()
+    for read, write in zip(reads, writes):
+        read.wait()
+        write.start()
+    for write in writes:
+        write.wait()
 
 
 def shards(
@@ -410,17 +433,21 @@
             pltpu.VMEM((blocks * 3,) + square, F32),
             pltpu.VMEM((slots + 1,) + square, F32),
             pltpu.SMEM((slots,), jnp.int32),
+            pltpu.SMEM((blocks * 3 + 1,), jnp.int32),
             pltpu.VMEM((blocks, 3) + square, BF16),
             pltpu.VMEM((blocks, 3) + square, BF16),
-            pltpu.VMEM((3, size, blocks * size), BF16),
-            pltpu.VMEM((3, size, blocks * size), BF16),
+            pltpu.VMEM((blocks, 3) + square, BF16),
+            pltpu.VMEM((blocks, 3) + square, BF16),
             pltpu.VMEM(square, F32),
             pltpu.VMEM(square, F32),
             pltpu.VMEM(square, F32),
-            pltpu.VMEM((chips,) + square, F32),
+            pltpu.VMEM((chips,) + square, BF16),
             pltpu.VMEM((blocks,) + square, F32),
-            pltpu.VMEM((2, n_user, piece, size), sent),
-            pltpu.VMEM((2, n_user, piece, size), sent),
+            pltpu.VMEM((3,) + square, F32),
+            pltpu.VMEM((n_user, piece, size), sent),
+            pltpu.VMEM((n_user, piece, size), sent),
+            pltpu.VMEM((n_user, piece, size), F32),
+            pltpu.VMEM((n_user, piece, size), F32),
             pltpu.VMEM((n_user, piece, size), F32),
             pltpu.VMEM((piece, size), F32),
             pltpu.VMEM((n_user, piece, size), sent),
@@ -461,7 +488,11 @@
         ),
         in_specs=[hbm] * 2,
         out_specs=(hbm, hbm),
-        scratch_shapes=[dma((blocks + 1,))],
+        scratch_shapes=[
+            pltpu.VMEM(sketch.shape, F32),
+            pltpu.VMEM(second.shape, F32),
+            dma((2, 2 * blocks + 1)),
+        ],
         compiler_params=pltpu.CompilerParams(vmem_limit_bytes=63 * 1024 * 1024),
     )(sketch, second)
     return sketch.reshape(blocks * size, size), second

time: 51.8 us -> 32.8 us (0.63)
  Pallas kernels: 50.4 us -> 31.4 us
    pallas_call x1, Pallas kernels: 18 us -> 1.86 us  [shards(): pl.pallas_call(hand_over, out_shape=(jax.ShapeDtypeStruct(sketch.shape, F...]
    pallas_call x1, Pallas kernels: 32.4 us -> 29.5 us  [shards(): pl.pallas_call(functools.partial(kernel, n_user, n_item, scale), out_shap...]
where the time goes in v3:
time: 32.8 us; the launch traced here: 32.7 us
  Pallas kernels  31.4 us (96%)
  between operations  1.29 us (4%)
    pallas_call x1, Pallas kernels, shards(): pl.pallas_call(functools.partial(kernel, n_user, n_item, scale), out_shap...  29.5 us
    pallas_call x1, Pallas kernels, shards(): pl.pallas_call(hand_over, out_shape=(jax.ShapeDtypeStruct(sketch.shape, F...  1.86 us

profile of v3, /device:TPU:0, one launch (start us, length us, event | category | flops | bytes accessed | tf_op | source)
XLA Modules:
  0.0 32.7 jit_solution(3336481741225812834)
XLA Ops:
  1.3 29.5 %shard_map.104 = (f32[2,256,256]{2,1,0:T(8,128)}, f32[1,32,256]{2,1,0:T(8,128)}) custom-call(s32[1,8,24]{2,1,0:T(8,128)} %bitcast.3, s32[1,8,24]{2,1,0:T(8,128)} %bitcast.4, s32[1,24]{1,0:T(1,128)} %tile_row_hbm.1, s32[1,24]{1,0:T(1,128)} %tile_col_hbm.1, s32[1,1]{1,0:T(1,128)S(6)} %copy.11.tile_count_hbm, bf16[512,256]{1,0:T(8,128)(2,1)} %user_hbm.1, ...), custom_call_target="tpu_custom_call" | custom-call | tf_op jit(solution)/shard_map/pallas_call | solution.py:414
  30.8 1.9 %shard_map.105 = (f32[2,256,256]{2,1,0:T(8,128)}, f32[1,32,256]{2,1,0:T(8,128)}) custom-call(f32[2,256,256]{2,1,0:T(8,128)} %get-tuple-element.6.sketch, f32[1,32,256]{2,1,0:T(8,128)} %get-tuple-element.7.second), custom_call_target="tpu_custom_call" | custom-call | tf_op jit(solution)/shard_map/pallas_call | solution.py:483

commit v4 on v3

--- a/solution.py
+++ b/solution.py
@@ -136,20 +136,28 @@
         )
     pl.semaphore_wait(barrier, 2 + (chips - 1) + (n_user - 1))
 
-    panel_copies = []
-    for which, (source, target) in enumerate(((item_hbm, v_all), (test_hbm, t_all))):
-        for side, (window, device) in enumerate(((near_window, far_item), (far_window, partner))):
-            panel_copies.append(
-                pltpu.make_async_remote_copy(
-                    src_ref=source,
-                    dst_ref=target.at[window],
-                    send_sem=panel_send_sem.at[which, side],
-                    recv_sem=panel_recv_sem.at[which, side],
-                    device_id={"item": device},
-                    device_id_type=MESH,
-                )
-            )
-            panel_copies[-1].start()
+    half = size // 2
+    panel_copies = [
+        pltpu.make_async_remote_copy(
+            src_ref=source.at[pl.ds(start, count)],
+            dst_ref=target.at[window, pl.ds(start, count)],
+            send_sem=panel_send_sem.at[n],
+            recv_sem=panel_recv_sem.at[n],
+            device_id={"item": device},
+            device_id_type=MESH,
+        )
+        for n, (source, target, window, device, start, count) in enumerate(
+            (
+                (item_hbm, v_all, near_window, far_item, 0, half),
+                (item_hbm, v_all, far_window, partner, 0, size),
+                (item_hbm, v_all, near_window, far_item, half, half),
+                (test_hbm, t_all, near_window, far_item, 0, size),
+                (test_hbm, t_all, far_window, partner, 0, size),
+            )
+        )
+    ]
+    for copy in panel_copies:
+        copy.start()
 
     for copy in small_copies:
         copy.wait()
@@ -171,7 +179,7 @@
             masks[t, s * strip : (s + 1) * strip, :] = seen.astype(F32).astype(BF16)
         return carry
 
-    lax.fori_loop(0, slots, make_mask, 0)
+    lax.fori_loop(0, slots, make_mask, 0, unroll=2)
 
     stride = 1 << (slots - 1).bit_length()
     order = []
@@ -185,35 +193,46 @@
     for group in range(blocks * 3 + 1):
         bounds[group] = sum((key < group * stride).astype(jnp.int32) for key in order)
 
-    def predict(window):
+    def predict(window, h):
         product = lax.dot_general(
-            user_ref[...], v_all[window], (((1,), (1,)), ((), ())), preferred_element_type=F32
+            user_ref[...],
+            v_all[window, h * half : (h + 1) * half],
+            (((1,), (1,)), ((), ())),
+            preferred_element_type=F32,
         )
         for r in range(blocks):
-            p_buf[r * 3 + window] = product[r * size : (r + 1) * size]
+            p_buf[h, r * 3 + window] = product[r * size : (r + 1) * size]
 
     prefix[0] = jnp.zeros((size, size), F32)
     u_copy.wait()
     v_copy.wait()
-    predict(1)
+    for h in range(2):
+        predict(1, h)
     panel_copies[1].wait_recv()
-    predict(near_window)
+    for h in range(2):
+        predict(near_window, h)
     x_copy.wait()
-    panel_copies[0].wait_recv()
-    predict(far_window)
-
-    def add_tile(i, carry):
-        key = keys[i]
-        t = jnp.bitwise_and(key, stride - 1)
-        group = lax.shift_right_logical(key, stride.bit_length() - 1)
-        for s in range(size // strip):
-            at = slice(s * strip, (s + 1) * strip)
-            gap = x_buf[t, at, :].astype(F32) - p_buf[group, at, :]
-            residue = gap.astype(BF16) * masks[t, at, :]
-            prefix[i + 1, at, :] = prefix[i, at, :] + residue.astype(F32)
-        return carry
-
-    lax.fori_loop(0, slots, add_tile, 0)
+
+    for h in range(2):
+        panel_copies[2 * h].wait_recv()
+        predict(far_window, h)
+        columns = slice(h * half, (h + 1) * half)
+
+        def add_tile(i, sums):
+            key = keys[i]
+            t = jnp.bitwise_and(key, stride - 1)
+            group = lax.shift_right_logical(key, stride.bit_length() - 1)
+            new = []
+            for s, total in enumerate(sums):
+                at = slice(s * strip, (s + 1) * strip)
+                gap = x_buf[t, at, columns].astype(F32) - p_buf[h, group, at, :]
+                residue = gap.astype(BF16) * masks[t, at, columns]
+                new.append(total + residue.astype(F32))
+                prefix[i + 1, at, columns] = new[-1]
+            return tuple(new)
+
+        zero = jnp.zeros((strip, half), F32)
+        lax.fori_loop(0, slots, add_tile, (zero,) * (size // strip), unroll=4)
 
     def group_sum(r, window):
         group = r * 3 + window
@@ -228,8 +247,8 @@
 
     split_sums(1 - core)
     t_copy.wait()
+    panel_copies[4].wait_recv()
     panel_copies[3].wait_recv()
-    panel_copies[2].wait_recv()
 
     def sketch_block(r):
         total = None
@@ -376,23 +395,15 @@
         copy.wait_send()
 
 
-def hand_over(sketch, second, sketch_out, second_out, sketch_buf, second_buf, sem):
-    triples = [(second, second_buf, second_out)]
-    half = sketch.shape[1] // 2
-    for r in range(sketch.shape[0]):
-        for h in range(2):
-            at = pl.ds(h * half, half)
-            triples.append((sketch.at[r, at], sketch_buf.at[r, at], sketch_out.at[r, at]))
-    reads, writes = [], []
-    for n, (source, buffer, target) in enumerate(triples):
-        reads.append(pltpu.make_async_copy(source, buffer, sem.at[0, n]))
-        writes.append(pltpu.make_async_copy(buffer, target, sem.at[1, n]))
-        reads[-1].start()
-    for read, write in zip(reads, writes):
-        read.wait()
-        write.start()
-    for write in writes:
-        write.wait()
+def hand_over(sketch, second, sketch_out, second_out, sem):
+    copies = [
+        pltpu.make_async_copy(second, second_out, sem.at[0]),
+        pltpu.make_async_copy(sketch, sketch_out, sem.at[1]),
+    ]
+    for copy in copies:
+        copy.start()
+    for copy in copies:
+        copy.wait()
 
 
 def shards(
@@ -414,11 +425,11 @@
     sketch, second = pl.pallas_call(
         functools.partial(kernel, n_user, n_item, scale),
         out_shape=(
-            jax.ShapeDtypeStruct((blocks,) + square, F32),
-            jax.ShapeDtypeStruct((1, piece, size), F32),
+            pltpu.VMEM((blocks,) + square, F32),
+            pltpu.VMEM((1, piece, size), F32),
         ),
         in_specs=[hbm] * 9,
-        out_specs=(hbm, vmem),
+        out_specs=(vmem, vmem),
         scratch_shapes=[
             pltpu.SMEM((1, words, slots), jnp.int32),
             pltpu.SMEM((1, words, slots), jnp.int32),
@@ -430,7 +441,7 @@
             pltpu.VMEM((slots,) + square, BF16),
             pltpu.VMEM((3,) + square, BF16),
             pltpu.VMEM((3,) + square, BF16),
-            pltpu.VMEM((blocks * 3,) + square, F32),
+            pltpu.VMEM((2, blocks * 3, size, size // 2), F32),
             pltpu.VMEM((slots + 1,) + square, F32),
             pltpu.SMEM((slots,), jnp.int32),
             pltpu.SMEM((blocks * 3 + 1,), jnp.int32),
@@ -453,8 +464,8 @@
             pltpu.VMEM((n_user, piece, size), sent),
             pltpu.VMEM((n_user - 1, piece, size), sent),
             dma((10,)),
-            dma((2, 2)),
-            dma((2, 2)),
+            dma((5,)),
+            dma((5,)),
             dma((CHUNKS,)),
             dma((CHUNKS,)),
             dma((CHUNKS, chips - 1)),
@@ -467,18 +478,25 @@
             dma((n_user - 1,)),
         ],
         compiler_params=pltpu.CompilerParams(
-            collective_id=0, has_side_effects=True, vmem_limit_bytes=63 * 1024 * 1024
+            collective_id=0, has_side_effects=True, vmem_limit_bytes=48 * 1024 * 1024
         ),
     )(
-        jnp.swapaxes(row_bits, 1, 2),
-        jnp.swapaxes(col_bits, 1, 2),
-        tile_row,
-        tile_col,
-        tile_count,
-        user_panel,
-        xtiles,
-        item_panel,
-        test_panel,
+        *(
+            operand
+            if operand.size == 1
+            else pltpu.with_memory_space_constraint(operand, pltpu.HBM)
+            for operand in (
+                jnp.swapaxes(row_bits, 1, 2),
+                jnp.swapaxes(col_bits, 1, 2),
+                tile_row,
+                tile_col,
+                tile_count,
+                user_panel,
+                xtiles,
+                item_panel,
+                test_panel,
+            )
+        )
     )
     sketch, second = pl.pallas_call(
         hand_over,
@@ -486,14 +504,12 @@
             jax.ShapeDtypeStruct(sketch.shape, F32),
             jax.ShapeDtypeStruct(second.shape, F32),
         ),
-        in_specs=[hbm] * 2,
+        in_specs=[vmem] * 2,
         out_specs=(hbm, hbm),
         scratch_shapes=[
-            pltpu.VMEM(sketch.shape, F32),
-            pltpu.VMEM(second.shape, F32),
-            dma((2, 2 * blocks + 1)),
+            dma((2,)),
         ],
-        compiler_params=pltpu.CompilerParams(vmem_limit_bytes=63 * 1024 * 1024),
+        compiler_params=pltpu.CompilerParams(vmem_limit_bytes=1024 * 1024),
     )(sketch, second)
     return sketch.reshape(blocks * size, size), second
 

time: 32.8 us -> 31.2 us (0.951)
  Pallas kernels: 31.4 us -> 29.7 us
    pallas_call x1, Pallas kernels: 1.86 us -> 0.82 us  [shards(): pl.pallas_call(hand_over, out_shape=(jax.ShapeDtypeStruct(sketch.shape, F...]
    pallas_call x1, Pallas kernels: 29.5 us -> 28.9 us  [shards(): pl.pallas_call(functools.partial(kernel, n_user, n_item, scale), out_shap...]
where the time goes in v4:
time: 31.2 us; the launch traced here: 31 us
  Pallas kernels  29.7 us (95%)
  between operations  1.29 us (4%)
    pallas_call x1, Pallas kernels, shards(): pl.pallas_call(functools.partial(kernel, n_user, n_item, scale), out_shap...  28.9 us
    pallas_call x1, Pallas kernels, shards(): pl.pallas_call(hand_over, out_shape=(jax.ShapeDtypeStruct(sketch.shape, F...  0.82 us

profile of v4, /device:TPU:0, one launch (start us, length us, event | category | flops | bytes accessed | tf_op | source)
XLA Modules:
  0.0 31.0 jit_solution(12144857043708070712)
XLA Ops:
  1.3 28.9 %shard_map.104 = (f32[2,256,256]{2,1,0:T(8,128)S(1)}, f32[1,32,256]{2,1,0:T(8,128)S(1)}) custom-call(s32[1,8,24]{2,1,0:T(8,128)} %bitcast.3, s32[1,8,24]{2,1,0:T(8,128)} %bitcast.4, s32[1,24]{1,0:T(1,128)} %tile_row_hbm.1, s32[1,24]{1,0:T(1,128)} %tile_col_hbm.1, s32[1,1]{1,0:T(1,128)S(6)} %copy.11.tile_count_hbm, bf16[512,256]{1,0:T(8,128)(2,1)} %user_hbm.1, ...), custom_call_target="tpu_custom_call" | custom-call | tf_op jit(solution)/shard_map/pallas_call | solution.py:425
  30.2 0.8 %shard_map.105 = (f32[2,256,256]{2,1,0:T(8,128)}, f32[1,32,256]{2,1,0:T(8,128)}) custom-call(f32[2,256,256]{2,1,0:T(8,128)S(1)} %get-tuple-element.6.sketch, f32[1,32,256]{2,1,0:T(8,128)S(1)} %get-tuple-element.7.second), custom_call_target="tpu_custom_call" | custom-call | tf_op jit(solution)/shard_map/pallas_call | solution.py:501

commit v5 on v4

--- a/solution.py
+++ b/solution.py
@@ -28,6 +28,10 @@
             k //= 2
         p *= 2
     return [(a, b) for a, b in pairs if b < length]
+
+
+def wrapped(index, size):
+    return jnp.where(index >= size, index - size, index)
 
 
 def kernel(
@@ -52,7 +56,8 @@
     tile_count,
     user_ref,
     x_buf,
-    masks,
+    row_masks,
+    col_masks,
     v_all,
     t_all,
     p_buf,
@@ -98,8 +103,8 @@
     chips = n_item // 2
     slots, size = x_buf.shape[0], x_buf.shape[1]
     blocks = user_ref.shape[0] // size
-    lower = lax.rem(item + n_item - 1, n_item)
-    upper = lax.rem(item + 1, n_item)
+    lower = wrapped(item + n_item - 1, n_item)
+    upper = wrapped(item + 1, n_item)
     partner = chip * 2 + 1 - core
     far_window = 2 * core
     near_window = 2 - far_window
@@ -128,11 +133,11 @@
     pl.semaphore_signal(barrier, inc=1, device_id={"item": far_item}, device_id_type=MESH)
     pl.semaphore_signal(barrier, inc=1, device_id={"item": partner}, device_id_type=MESH)
     for d in range(1, chips):
-        other = lax.rem(chip + d, chips) * 2 + core
+        other = wrapped(chip + d, chips) * 2 + core
         pl.semaphore_signal(barrier, inc=1, device_id={"item": other}, device_id_type=MESH)
     for d in range(1, n_user):
         pl.semaphore_signal(
-            barrier, inc=1, device_id={"user": lax.rem(user + d, n_user)}, device_id_type=MESH
+            barrier, inc=1, device_id={"user": wrapped(user + d, n_user)}, device_id_type=MESH
         )
     pl.semaphore_wait(barrier, 2 + (chips - 1) + (n_user - 1))
 
@@ -163,28 +168,27 @@
         copy.wait()
     strip = 16
     lanes = lax.broadcasted_iota(jnp.int32, (strip, size), 1)
-    rows = lax.broadcasted_iota(jnp.int32, (strip, size), 0)
+    rows = lax.broadcasted_iota(jnp.int32, (strip, half), 0)
 
     def make_mask(t, carry):
         live = (t < tile_count[0, 0]).astype(jnp.int32)
         words = jnp.zeros((strip, size), jnp.int32)
         for w in range(size // 32):
             words = jnp.where(lanes // 32 == w, col_bits[0, w, t] * live, words)
-        col_seen = jnp.bitwise_and(lax.shift_right_logical(words, jnp.bitwise_and(lanes, 31)), 1)
+        seen = jnp.bitwise_and(lax.shift_right_logical(words, jnp.bitwise_and(lanes, 31)), 1)
+        col_masks[t] = seen.astype(F32).astype(BF16)
         for s in range(size // strip):
-            word = jnp.full((strip, size), row_bits[0, s * strip // 32, t], jnp.int32)
-            seen = jnp.bitwise_and(
-                lax.shift_right_logical(word, rows + (s * strip) % 32), col_seen
-            )
-            masks[t, s * strip : (s + 1) * strip, :] = seen.astype(F32).astype(BF16)
+            word = jnp.full((strip, half), row_bits[0, s * strip // 32, t], jnp.int32)
+            seen = jnp.bitwise_and(lax.shift_right_logical(word, rows + (s * strip) % 32), 1)
+            row_masks[t, s * strip : (s + 1) * strip, :] = seen.astype(F32).astype(BF16)
         return carry
 
-    lax.fori_loop(0, slots, make_mask, 0, unroll=2)
+    lax.fori_loop(0, slots, make_mask, 0, unroll=4)
 
     stride = 1 << (slots - 1).bit_length()
     order = []
     for t in range(slots):
-        window = lax.rem(tile_col[0, t] - item + 1 + n_item, n_item)
+        window = wrapped(wrapped(tile_col[0, t] - item + 1 + n_item, n_item), n_item)
         order.append((tile_row[0, t] * 3 + window) * stride + t)
     for a, b in sorting_pairs(slots):
         order[a], order[b] = jnp.minimum(order[a], order[b]), jnp.maximum(order[a], order[b])
@@ -222,11 +226,12 @@
             key = keys[i]
             t = jnp.bitwise_and(key, stride - 1)
             group = lax.shift_right_logical(key, stride.bit_length() - 1)
+            col_mask = col_masks[t, :, columns]
             new = []
             for s, total in enumerate(sums):
                 at = slice(s * strip, (s + 1) * strip)
                 gap = x_buf[t, at, columns].astype(F32) - p_buf[h, group, at, :]
-                residue = gap.astype(BF16) * masks[t, at, columns]
+                residue = gap.astype(BF16) * (row_masks[t, at, :] * col_mask)
                 new.append(total + residue.astype(F32))
                 prefix[i + 1, at, columns] = new[-1]
             return tuple(new)
@@ -289,7 +294,7 @@
                     dst_ref=gathered.at[chip, at],
                     send_sem=chip_send_sem.at[j, d - 1],
                     recv_sem=chip_recv_sem.at[j, d - 1],
-                    device_id={"item": lax.rem(chip + d, chips) * 2 + core},
+                    device_id={"item": wrapped(chip + d, chips) * 2 + core},
                     device_id_type=MESH,
                 )
             )
@@ -347,7 +352,7 @@
     ):
         z_send[...] = term(window).astype(z_send.dtype)
         for n, d in enumerate(turns):
-            target = lax.rem(user + d, n_user)
+            target = wrapped(user + d, n_user)
             z_copies[side].append(
                 pltpu.make_async_remote_copy(
                     src_ref=z_send.at[target],
@@ -363,7 +368,7 @@
 
     piece_copies = []
     for n, d in enumerate(turns):
-        target = lax.rem(user + d, n_user)
+        target = wrapped(user + d, n_user)
         z_copies[1][n].wait_recv()
         z_copies[0][n].wait_recv()
         total = z_own[target] + near_recv[target] + far_recv[target].astype(F32)
@@ -438,7 +443,8 @@
             pltpu.SMEM((1, 1), jnp.int32),
             pltpu.VMEM(user_panel.shape, BF16),
             pltpu.VMEM((slots,) + square, BF16),
-            pltpu.VMEM((slots,) + square, BF16),
+            pltpu.VMEM((slots, size, size // 2), BF16),
+            pltpu.VMEM((slots, 16, size), BF16),
             pltpu.VMEM((3,) + square, BF16),
             pltpu.VMEM((3,) + square, BF16),
             pltpu.VMEM((2, blocks * 3, size, size // 2), F32),

time: 31.2 us -> 31.2 us (level)
  no operation moved by 1% of the time
where the time goes in v5:
time: 31.2 us; the launch traced here: 31 us
  Pallas kernels  29.7 us (95%)
  between operations  1.29 us (4%)
    pallas_call x1, Pallas kernels, shards(): pl.pallas_call(functools.partial(kernel, n_user, n_item, scale), out_shap...  28.9 us
    pallas_call x1, Pallas kernels, shards(): pl.pallas_call(hand_over, out_shape=(jax.ShapeDtypeStruct(sketch.shape, F...  0.82 us

profile of v5, /device:TPU:0, one launch (start us, length us, event | category | flops | bytes accessed | tf_op | source)
XLA Modules:
  0.0 31.0 jit_solution(5627680924835332647)
XLA Ops:
  1.3 28.9 %shard_map.104 = (f32[2,256,256]{2,1,0:T(8,128)S(1)}, f32[1,32,256]{2,1,0:T(8,128)S(1)}) custom-call(s32[1,8,24]{2,1,0:T(8,128)} %bitcast.3, s32[1,8,24]{2,1,0:T(8,128)} %bitcast.4, s32[1,24]{1,0:T(1,128)} %tile_row_hbm.1, s32[1,24]{1,0:T(1,128)} %tile_col_hbm.1, s32[1,1]{1,0:T(1,128)S(6)} %copy.11.tile_count_hbm, bf16[512,256]{1,0:T(8,128)(2,1)} %user_hbm.1, ...), custom_call_target="tpu_custom_call" | custom-call | tf_op jit(solution)/shard_map/pallas_call | solution.py:430
  30.2 0.8 %shard_map.105 = (f32[2,256,256]{2,1,0:T(8,128)}, f32[1,32,256]{2,1,0:T(8,128)}) custom-call(f32[2,256,256]{2,1,0:T(8,128)S(1)} %get-tuple-element.6.sketch, f32[1,32,256]{2,1,0:T(8,128)S(1)} %get-tuple-element.7.second), custom_call_target="tpu_custom_call" | custom-call | tf_op jit(solution)/shard_map/pallas_call | solution.py:507

commit v6 on v5

--- a/solution.py
+++ b/solution.py
@@ -142,27 +142,35 @@
     pl.semaphore_wait(barrier, 2 + (chips - 1) + (n_user - 1))
 
     half = size // 2
-    panel_copies = [
-        pltpu.make_async_remote_copy(
-            src_ref=source.at[pl.ds(start, count)],
-            dst_ref=target.at[window, pl.ds(start, count)],
-            send_sem=panel_send_sem.at[n],
-            recv_sem=panel_recv_sem.at[n],
-            device_id={"item": device},
-            device_id_type=MESH,
-        )
-        for n, (source, target, window, device, start, count) in enumerate(
-            (
-                (item_hbm, v_all, near_window, far_item, 0, half),
-                (item_hbm, v_all, far_window, partner, 0, size),
-                (item_hbm, v_all, near_window, far_item, half, half),
-                (test_hbm, t_all, near_window, far_item, 0, size),
-                (test_hbm, t_all, far_window, partner, 0, size),
-            )
-        )
-    ]
-    for copy in panel_copies:
-        copy.start()
+    parity = lax.rem(user, 2)
+    buddy = user + 1 - 2 * parity
+    halves = [pl.ds(pl.multiple_of(h * half, half), half) for h in (parity, 1 - parity)]
+    panel_copies = []
+
+    def panel_copy(source, target, device):
+        n = len(panel_copies)
+        panel_copies.append(
+            pltpu.make_async_remote_copy(
+                src_ref=source,
+                dst_ref=target,
+                send_sem=panel_send_sem.at[n],
+                recv_sem=panel_recv_sem.at[n],
+                device_id=device,
+                device_id_type=MESH,
+            )
+        )
+        panel_copies[-1].start()
+        return panel_copies[-1]
+
+    far_device, near_device = {"item": far_item}, {"item": partner}
+    far_v = panel_copy(item_hbm.at[halves[0]], v_all.at[near_window, halves[0]], far_device)
+    near_v = panel_copy(item_hbm, v_all.at[far_window], near_device)
+    far_t = panel_copy(test_hbm.at[halves[0]], t_all.at[near_window, halves[0]], far_device)
+    near_t = panel_copy(test_hbm, t_all.at[far_window], near_device)
+
+    def swap(panels):
+        block = panels.at[far_window, halves[0]]
+        return panel_copy(block, block, {"user": buddy})
 
     for copy in small_copies:
         copy.wait()
@@ -200,7 +208,7 @@
     def predict(window, h):
         product = lax.dot_general(
             user_ref[...],
-            v_all[window, h * half : (h + 1) * half],
+            v_all[window, halves[h]],
             (((1,), (1,)), ((), ())),
             preferred_element_type=F32,
         )
@@ -212,15 +220,20 @@
     v_copy.wait()
     for h in range(2):
         predict(1, h)
-    panel_copies[1].wait_recv()
+    near_v.wait_recv()
     for h in range(2):
         predict(near_window, h)
+    far_v.wait_recv()
+    swapped_v = swap(v_all)
     x_copy.wait()
 
     for h in range(2):
-        panel_copies[2 * h].wait_recv()
+        if h == 1:
+            far_t.wait_recv()
+            swapped_t = swap(t_all)
+            swapped_v.wait_recv()
         predict(far_window, h)
-        columns = slice(h * half, (h + 1) * half)
+        columns = halves[h]
 
         def add_tile(i, sums):
             key = keys[i]
@@ -252,8 +265,8 @@
 
     split_sums(1 - core)
     t_copy.wait()
-    panel_copies[4].wait_recv()
-    panel_copies[3].wait_recv()
+    near_t.wait_recv()
+    swapped_t.wait_recv()
 
     def sketch_block(r):
         total = None
@@ -470,8 +483,8 @@
             pltpu.VMEM((n_user, piece, size), sent),
             pltpu.VMEM((n_user - 1, piece, size), sent),
             dma((10,)),
-            dma((5,)),
-            dma((5,)),
+            dma((6,)),
+            dma((6,)),
             dma((CHUNKS,)),
             dma((CHUNKS,)),
             dma((CHUNKS, chips - 1)),

time: 31.2 us -> 32.1 us (1.029)
  Pallas kernels: 29.7 us -> 30.7 us
    pallas_call x1, Pallas kernels: 28.9 us -> 29.9 us  [shards(): pl.pallas_call(functools.partial(kernel, n_user, n_item, scale), out_shap...]
where the time goes in v6:
time: 32.1 us; the launch traced here: 32 us
  Pallas kernels  30.7 us (96%)
  between operations  1.29 us (4%)
    pallas_call x1, Pallas kernels, shards(): pl.pallas_call(functools.partial(kernel, n_user, n_item, scale), out_shap...  29.9 us
    pallas_call x1, Pallas kernels, shards(): pl.pallas_call(hand_over, out_shape=(jax.ShapeDtypeStruct(sketch.shape, F...  0.82 us

profile of v6, /device:TPU:0, one launch (start us, length us, event | category | flops | bytes accessed | tf_op | source)
XLA Modules:
  0.0 32.0 jit_solution(2414245539516535879)
XLA Ops:
  1.3 29.9 %shard_map.104 = (f32[2,256,256]{2,1,0:T(8,128)S(1)}, f32[1,32,256]{2,1,0:T(8,128)S(1)}) custom-call(s32[1,8,24]{2,1,0:T(8,128)} %bitcast.3, s32[1,8,24]{2,1,0:T(8,128)} %bitcast.4, s32[1,24]{1,0:T(1,128)} %tile_row_hbm.1, s32[1,24]{1,0:T(1,128)} %tile_col_hbm.1, s32[1,1]{1,0:T(1,128)S(6)} %copy.11.tile_count_hbm, bf16[512,256]{1,0:T(8,128)(2,1)} %user_hbm.1, ...), custom_call_target="tpu_custom_call" | custom-call | tf_op jit(solution)/shard_map/pallas_call | solution.py:443
  31.1 0.8 %shard_map.105 = (f32[2,256,256]{2,1,0:T(8,128)}, f32[1,32,256]{2,1,0:T(8,128)}) custom-call(f32[2,256,256]{2,1,0:T(8,128)S(1)} %get-tuple-element.6.sketch, f32[1,32,256]{2,1,0:T(8,128)S(1)} %get-tuple-element.7.second), custom_call_target="tpu_custom_call" | custom-call | tf_op jit(solution)/shard_map/pallas_call | solution.py:520

commit v7 on v5

--- a/solution.py
+++ b/solution.py
@@ -66,8 +66,8 @@
     bounds,
     a_hi,
     a_lo,
-    at_hi,
-    at_lo,
+    at_both,
+    s_part,
     half_send,
     half_recv,
     own_half,
@@ -243,25 +243,31 @@
         group = r * 3 + window
         return prefix[bounds[group + 1]] - prefix[bounds[group]]
 
-    def split_sums(r):
+    for r in (1 - core, core):
         for window in range(3):
             total = group_sum(r, window)
             high = total.astype(BF16)
-            a_hi[r, window] = high
-            a_lo[r, window] = (total - high.astype(F32)).astype(BF16)
-
-    split_sums(1 - core)
+            columns = slice(window * size, (window + 1) * size)
+            a_hi[r, :, columns] = high
+            a_lo[r, :, columns] = (total - high.astype(F32)).astype(BF16)
+
+    def products(r, columns, panel):
+        return jnp.dot(a_hi[r, :, columns], panel, preferred_element_type=F32) + jnp.dot(
+            a_lo[r, :, columns], panel, preferred_element_type=F32
+        )
+
     t_copy.wait()
     panel_copies[4].wait_recv()
+    first = near_window // 2
+    pair = pl.ds(pl.multiple_of(first * size, size), 2 * size)
+    panel = t_all[pl.ds(first, 2)].reshape(2 * size, size)
+    for r in (1 - core, core):
+        s_part[r] = products(r, pair, panel)
     panel_copies[3].wait_recv()
 
     def sketch_block(r):
-        total = None
-        for window in range(3):
-            for part in (a_hi, a_lo):
-                term = jnp.dot(part[r, window], t_all[window], preferred_element_type=F32)
-                total = term if total is None else total + term
-        return total
+        far = pl.ds(pl.multiple_of(far_window * size, size), size)
+        return s_part[r] + products(r, far, t_all[far_window])
 
     step = size // CHUNKS
     half_send[...] = sketch_block(1 - core)
@@ -279,7 +285,6 @@
             )
         )
         half_copies[-1].start()
-    split_sums(core)
     own_half[...] = sketch_block(core)
 
     chip_copies = []
@@ -304,8 +309,8 @@
         for window in range(3):
             turned = group_sum(r, window).T
             high = turned.astype(BF16)
-            at_hi[r, window] = high
-            at_lo[r, window] = (turned - high.astype(F32)).astype(BF16)
+            at_both[r, window, :, :size] = high
+            at_both[r, window, :, size:] = (turned - high.astype(F32)).astype(BF16)
 
     y_copies = []
     for j in range(CHUNKS):
@@ -328,8 +333,10 @@
         )
         y_copies[-1].start()
     def second(r, window, y_half):
-        return jnp.dot(at_hi[r, window], y_half, preferred_element_type=F32) + jnp.dot(
-            at_lo[r, window], y_half, preferred_element_type=F32
+        return jnp.dot(
+            at_both[r, window],
+            jnp.concatenate([y_half, y_half], axis=0),
+            preferred_element_type=F32,
         )
 
     y_half = y_full[core].astype(BF16)
@@ -346,32 +353,40 @@
 
     piece = size // n_user
     turns = sorted(range(1, n_user), key=lambda d: -min(d, n_user - d)) + [0]
-    z_copies = [[], []]
-    for side, (window, device, z_send, z_recv) in enumerate(
-        ((far_window, far_item, far_send, far_recv), (near_window, partner, near_send, near_recv))
-    ):
-        z_send[...] = term(window).astype(z_send.dtype)
-        for n, d in enumerate(turns):
-            target = wrapped(user + d, n_user)
-            z_copies[side].append(
-                pltpu.make_async_remote_copy(
-                    src_ref=z_send.at[target],
-                    dst_ref=z_recv.at[target],
-                    send_sem=z_send_sem.at[side, n],
-                    recv_sem=z_recv_sem.at[side, n],
-                    device_id={"item": device},
-                    device_id_type=MESH,
-                )
-            )
-            z_copies[side][-1].start()
+    far_send[...] = term(far_window).astype(far_send.dtype)
+    z_copies = []
+    for n, d in enumerate(turns):
+        target = wrapped(user + d, n_user)
+        z_copies.append(
+            pltpu.make_async_remote_copy(
+                src_ref=far_send.at[target],
+                dst_ref=far_recv.at[target],
+                send_sem=z_send_sem.at[n],
+                recv_sem=z_recv_sem.at[n],
+                device_id={"item": far_item},
+                device_id_type=MESH,
+            )
+        )
+        z_copies[-1].start()
+    near_send[...] = term(near_window)
+    near_copy = pltpu.make_async_remote_copy(
+        src_ref=near_send,
+        dst_ref=near_recv,
+        send_sem=z_send_sem.at[n_user],
+        recv_sem=z_recv_sem.at[n_user],
+        device_id={"item": partner},
+        device_id_type=MESH,
+    )
+    near_copy.start()
     z_own[...] = term(1)
 
+    near_copy.wait_recv()
+    z_own[...] = z_own[...] + near_recv[...]
     piece_copies = []
     for n, d in enumerate(turns):
         target = wrapped(user + d, n_user)
-        z_copies[1][n].wait_recv()
-        z_copies[0][n].wait_recv()
-        total = z_own[target] + near_recv[target] + far_recv[target].astype(F32)
+        z_copies[n].wait_recv()
+        total = z_own[target] + far_recv[target].astype(F32)
         if d == 0:
             piece_own[...] = total
             continue
@@ -394,7 +409,7 @@
     second_out[0] = total * scale
 
     out_copy.wait()
-    for copy in panel_copies + half_copies + chip_copies + y_copies + z_copies[0] + z_copies[1]:
+    for copy in panel_copies + half_copies + chip_copies + y_copies + z_copies + [near_copy]:
         copy.wait_send()
     for copy in piece_copies:
         copy.wait_send()
@@ -451,10 +466,10 @@
             pltpu.VMEM((slots + 1,) + square, F32),
             pltpu.SMEM((slots,), jnp.int32),
             pltpu.SMEM((blocks * 3 + 1,), jnp.int32),
-            pltpu.VMEM((blocks, 3) + square, BF16),
-            pltpu.VMEM((blocks, 3) + square, BF16),
-            pltpu.VMEM((blocks, 3) + square, BF16),
-            pltpu.VMEM((blocks, 3) + square, BF16),
+            pltpu.VMEM((blocks, size, 3 * size), BF16),
+            pltpu.VMEM((blocks, size, 3 * size), BF16),
+            pltpu.VMEM((blocks, 3, size, 2 * size), BF16),
+            pltpu.VMEM((blocks,) + square, F32),
             pltpu.VMEM(square, F32),
             pltpu.VMEM(square, F32),
             pltpu.VMEM(square, F32),
@@ -478,8 +493,8 @@
             dma((CHUNKS, chips - 1)),
             dma((CHUNKS,)),
             dma((CHUNKS,)),
-            dma((2, n_user)),
-            dma((2, n_user)),
+            dma((n_user + 1,)),
+            dma((n_user + 1,)),
             dma((n_user - 1,)),
             dma((n_user - 1,)),
         ],

time: 31.2 us -> 30.7 us (0.984)
  Pallas kernels: 29.7 us -> 29.3 us
    pallas_call x1, Pallas kernels: 28.9 us -> 28.5 us  [shards(): pl.pallas_call(functools.partial(kernel, n_user, n_item, scale), out_shap...]
where the time goes in v7:
time: 30.7 us; the launch traced here: 30.6 us
  Pallas kernels  29.3 us (95%)
  between operations  1.29 us (4%)
    pallas_call x1, Pallas kernels, shards(): pl.pallas_call(functools.partial(kernel, n_user, n_item, scale), out_shap...  28.5 us
    pallas_call x1, Pallas kernels, shards(): pl.pallas_call(hand_over, out_shape=(jax.ShapeDtypeStruct(sketch.shape, F...  0.82 us

profile of v7, /device:TPU:0, one launch (start us, length us, event | category | flops | bytes accessed | tf_op | source)
XLA Modules:
  0.0 30.6 jit_solution(9297748511608761926)
XLA Ops:
  1.3 28.5 %shard_map.104 = (f32[2,256,256]{2,1,0:T(8,128)S(1)}, f32[1,32,256]{2,1,0:T(8,128)S(1)}) custom-call(s32[1,8,24]{2,1,0:T(8,128)} %bitcast.3, s32[1,8,24]{2,1,0:T(8,128)} %bitcast.4, s32[1,24]{1,0:T(1,128)} %tile_row_hbm.1, s32[1,24]{1,0:T(1,128)} %tile_col_hbm.1, s32[1,1]{1,0:T(1,128)S(6)} %copy.11.tile_count_hbm, bf16[512,256]{1,0:T(8,128)(2,1)} %user_hbm.1, ...), custom_call_target="tpu_custom_call" | custom-call | tf_op jit(solution)/shard_map/pallas_call | solution.py:445
  29.8 0.8 %shard_map.105 = (f32[2,256,256]{2,1,0:T(8,128)}, f32[1,32,256]{2,1,0:T(8,128)}) custom-call(f32[2,256,256]{2,1,0:T(8,128)S(1)} %get-tuple-element.6.sketch, f32[1,32,256]{2,1,0:T(8,128)S(1)} %get-tuple-element.7.second), custom_call_target="tpu_custom_call" | custom-call | tf_op jit(solution)/shard_map/pallas_call | solution.py:522

commit v8 on v7

--- a/solution.py
+++ b/solution.py
@@ -89,8 +89,8 @@
     half_recv_sem,
     chip_send_sem,
     chip_recv_sem,
-    y_send_sem,
-    y_recv_sem,
+    pair_send_sem,
+    pair_recv_sem,
     z_send_sem,
     z_recv_sem,
     piece_send_sem,
@@ -287,23 +287,31 @@
         half_copies[-1].start()
     own_half[...] = sketch_block(core)
 
+    def part_copy(source_chip, at, send_sem, recv_sem, device):
+        block = gathered.at[core, source_chip, at]
+        copy = pltpu.make_async_remote_copy(
+            src_ref=block,
+            dst_ref=block,
+            send_sem=send_sem,
+            recv_sem=recv_sem,
+            device_id={"item": device},
+            device_id_type=MESH,
+        )
+        copy.start()
+        return copy
+
     chip_copies = []
+    pair_copies = [[] for _ in range(CHUNKS)]
     for j in range(CHUNKS):
         at = pl.ds(j * step, step)
         half_copies[j].wait_recv()
-        gathered[chip, at, :] = (own_half[at, :] + half_recv[at, :]).astype(BF16)
+        gathered[core, chip, at, :] = (own_half[at, :] + half_recv[at, :]).astype(BF16)
         for d in range(1, chips):
-            chip_copies.append(
-                pltpu.make_async_remote_copy(
-                    src_ref=gathered.at[chip, at],
-                    dst_ref=gathered.at[chip, at],
-                    send_sem=chip_send_sem.at[j, d - 1],
-                    recv_sem=chip_recv_sem.at[j, d - 1],
-                    device_id={"item": wrapped(chip + d, chips) * 2 + core},
-                    device_id_type=MESH,
-                )
-            )
-            chip_copies[-1].start()
+            other = wrapped(chip + d, chips) * 2 + core
+            sems = chip_send_sem.at[j, d - 1], chip_recv_sem.at[j, d - 1]
+            chip_copies.append(part_copy(chip, at, *sems, other))
+        sems = pair_send_sem.at[j, 0], pair_recv_sem.at[j, 0]
+        pair_copies[j].append(part_copy(chip, at, *sems, partner))
 
     for r in range(blocks):
         for window in range(3):
@@ -312,26 +320,21 @@
             at_both[r, window, :, :size] = high
             at_both[r, window, :, size:] = (turned - high.astype(F32)).astype(BF16)
 
-    y_copies = []
     for j in range(CHUNKS):
         at = pl.ds(j * step, step)
         for d in range(1, chips):
             chip_copies[j * (chips - 1) + d - 1].wait_recv()
-        total = gathered[0, at, :].astype(F32)
+            sems = pair_send_sem.at[j, d], pair_recv_sem.at[j, d]
+            source_chip = wrapped(chip + chips - d, chips)
+            pair_copies[j].append(part_copy(source_chip, at, *sems, partner))
+
+    def add_parts(r):
+        total = gathered[r, 0].astype(F32)
         for other in range(1, chips):
-            total = total + gathered[other, at, :].astype(F32)
-        y_full[core, at, :] = total
-        y_copies.append(
-            pltpu.make_async_remote_copy(
-                src_ref=y_full.at[core, at],
-                dst_ref=y_full.at[core, at],
-                send_sem=y_send_sem.at[j],
-                recv_sem=y_recv_sem.at[j],
-                device_id={"item": partner},
-                device_id_type=MESH,
-            )
-        )
-        y_copies[-1].start()
+            total = total + gathered[r, other].astype(F32)
+        y_full[r] = total
+        return total.astype(BF16)
+
     def second(r, window, y_half):
         return jnp.dot(
             at_both[r, window],
@@ -339,14 +342,13 @@
             preferred_element_type=F32,
         )
 
-    y_half = y_full[core].astype(BF16)
+    y_half = add_parts(core)
     for window in range(3):
         z_part[window] = second(core, window, y_half)
     for j in range(CHUNKS):
-        y_copies[j].wait_recv()
-    out_copy = pltpu.make_async_copy(y_full, sketch_out, local_sem.at[3])
-    out_copy.start()
-    y_half = y_full[1 - core].astype(BF16)
+        for copy in pair_copies[j]:
+            copy.wait_recv()
+    y_half = add_parts(1 - core)
 
     def term(window):
         return (z_part[window] + second(1 - core, window, y_half)).reshape(n_user, piece, size)
@@ -368,6 +370,8 @@
             )
         )
         z_copies[-1].start()
+    out_copy = pltpu.make_async_copy(y_full, sketch_out, local_sem.at[3])
+    out_copy.start()
     near_send[...] = term(near_window)
     near_copy = pltpu.make_async_remote_copy(
         src_ref=near_send,
@@ -409,8 +413,11 @@
     second_out[0] = total * scale
 
     out_copy.wait()
-    for copy in panel_copies + half_copies + chip_copies + y_copies + z_copies + [near_copy]:
+    for copy in panel_copies + half_copies + chip_copies + z_copies + [near_copy]:
         copy.wait_send()
+    for copies in pair_copies:
+        for copy in copies:
+            copy.wait_send()
     for copy in piece_copies:
         copy.wait_send()
 
@@ -473,7 +480,7 @@
             pltpu.VMEM(square, F32),
             pltpu.VMEM(square, F32),
             pltpu.VMEM(square, F32),
-            pltpu.VMEM((chips,) + square, BF16),
+            pltpu.VMEM((blocks, chips) + square, BF16),
             pltpu.VMEM((blocks,) + square, F32),
             pltpu.VMEM((3,) + square, F32),
             pltpu.VMEM((n_user, piece, size), sent),
@@ -491,8 +498,8 @@
             dma((CHUNKS,)),
             dma((CHUNKS, chips - 1)),
             dma((CHUNKS, chips - 1)),
-            dma((CHUNKS,)),
-            dma((CHUNKS,)),
+            dma((CHUNKS, chips)),
+            dma((CHUNKS, chips)),
             dma((n_user + 1,)),
             dma((n_user + 1,)),
             dma((n_user - 1,)),

time: 30.7 us -> 30.7 us (level)
  no operation moved by 1% of the time
where the time goes in v8:
time: 30.7 us; the launch traced here: 30.6 us
  Pallas kernels  29.3 us (95%)
  between operations  1.29 us (4%)
    pallas_call x1, Pallas kernels, shards(): pl.pallas_call(functools.partial(kernel, n_user, n_item, scale), out_shap...  28.5 us
    pallas_call x1, Pallas kernels, shards(): pl.pallas_call(hand_over, out_shape=(jax.ShapeDtypeStruct(sketch.shape, F...  0.82 us

profile of v8, /device:TPU:0, one launch (start us, length us, event | category | flops | bytes accessed | tf_op | source)
XLA Modules:
  0.0 30.6 jit_solution(12978000223150478838)
XLA Ops:
  1.3 28.5 %shard_map.104 = (f32[2,256,256]{2,1,0:T(8,128)S(1)}, f32[1,32,256]{2,1,0:T(8,128)S(1)}) custom-call(s32[1,8,24]{2,1,0:T(8,128)} %bitcast.3, s32[1,8,24]{2,1,0:T(8,128)} %bitcast.4, s32[1,24]{1,0:T(1,128)} %tile_row_hbm.1, s32[1,24]{1,0:T(1,128)} %tile_col_hbm.1, s32[1,1]{1,0:T(1,128)S(6)} %copy.11.tile_count_hbm, bf16[512,256]{1,0:T(8,128)(2,1)} %user_hbm.1, ...), custom_call_target="tpu_custom_call" | custom-call | tf_op jit(solution)/shard_map/pallas_call | solution.py:452
  29.8 0.8 %shard_map.105 = (f32[2,256,256]{2,1,0:T(8,128)}, f32[1,32,256]{2,1,0:T(8,128)}) custom-call(f32[2,256,256]{2,1,0:T(8,128)S(1)} %get-tuple-element.6.sketch, f32[1,32,256]{2,1,0:T(8,128)S(1)} %get-tuple-element.7.second), custom_call_target="tpu_custom_call" | custom-call | tf_op jit(solution)/shard_map/pallas_call | solution.py:529
